TPU v7x, 128 devices: a whole 4x4x4 slice. The times are simulated.
128 devices in a mesh: ctx: 32 (over y, x_lo, z), fsdp: 4 (over x_hi, core).
Axes of the slice: x: 4 (x_hi: 2, x_lo: 2; x = x_hi * 2 + x_lo), y: 4, z: 4, core: 2. Of those that a mesh axis runs over, the one named last changes fastest.
Arguments:
- tokens: bfloat16 [4, 4096, 960], P('fsdp', 'ctx'), may hold values from -6 to 6
- pair_table: int32 [32], replicated, may hold values from 0 to 31, each once
- gain_attn: float32 [960], replicated, may hold values from 0.1 to 1.9
- w_query: bfloat16 [960, 960], P('fsdp', 'ctx'), may hold values from -0.1875 to 0.1875
- w_key: bfloat16 [960, 320], P('fsdp', 'ctx'), may hold values from -0.1875 to 0.1875
- w_value: bfloat16 [960, 320], P('fsdp', 'ctx'), may hold values from -0.1875 to 0.1875
- w_out: bfloat16 [960, 960], P('fsdp', 'ctx'), may hold values from -3.5 to 3.5
- gain_mlp: float32 [960], replicated, may hold values from 0.1 to 1.9
- w_gate: bfloat16 [960, 2560], P('fsdp', 'ctx'), may hold values from -0.1875 to 0.1875
- w_up: bfloat16 [960, 2560], P('fsdp', 'ctx'), may hold values from -0.1875 to 0.1875
- w_down: bfloat16 [2560, 960], P('fsdp', 'ctx'), may hold values from -0.125 to 0.125
- cotangent: bfloat16 [4, 4096, 960], P('fsdp', 'ctx'), may hold values from -6 to 6
Outputs:
- result: bfloat16 [4, 4096, 960], P('fsdp', 'ctx')
- grad_tokens: float32 [4, 4096, 960], P('fsdp', 'ctx')
- grad_gain_attn: float32 [960], replicated
- grad_w_query: float32 [960, 960], P('fsdp', 'ctx')
- grad_w_key: float32 [960, 320], P('fsdp', 'ctx')
- grad_w_value: float32 [960, 320], P('fsdp', 'ctx')
- grad_w_out: float32 [960, 960], P('fsdp', 'ctx')
- grad_gain_mlp: float32 [960], replicated
- grad_w_gate: float32 [960, 2560], P('fsdp', 'ctx')
- grad_w_up: float32 [960, 2560], P('fsdp', 'ctx')
- grad_w_down: float32 [2560, 960], P('fsdp', 'ctx')
Inputs may be any that keep to these rules, and one draw needn't show every extreme that they name: A permutation of the indices of ctx; index c holds the sequence blocks pair_table[c] and 63 - pair_table[c], each of 64 tokens.
All inputs are finite; a program needn't handle non-finite values.
Results may differ from a plain program's by a relative error of at most 0.035.
Values may be sent and summed in bfloat16 or wider, within the bound.
No kernel may reach another device: no remote copies, remote signals or barrier semaphores. Data moves between devices by JAX's collectives and lax.ppermute only.
A program may use at most 128 MiB of HBM per device.

v0:
```python
import math

import jax
import jax.numpy as jnp
from jax import lax
from jax.sharding import PartitionSpec as P

QUERY_HEADS = 15
KEY_VALUE_HEADS = 5
HEAD_WIDTH = 64


EPSILON = 1e-05
THETA = 10000.0
MASK_FLOOR = -1e30


def token_positions(pair_table, rows_per_block, ctx_count):
    sequence_length = rows_per_block * ctx_count
    row_index = jnp.arange(sequence_length, dtype=jnp.int32)
    owner_index = row_index // rows_per_block
    within = row_index % rows_per_block
    half_rows = rows_per_block // 2
    matches = (owner_index[:, None] == jnp.arange(ctx_count, dtype=jnp.int32)[None, :]).astype(
        jnp.int32
    )
    paired = jnp.sum(matches * pair_table[None, :], axis=1, dtype=jnp.int32)
    blocks = jnp.where(within < half_rows, paired, 2 * ctx_count - 1 - paired)
    return blocks * half_rows + within % half_rows


def rope_tables(positions, head_size):
    half_size = head_size // 2
    frequencies = THETA ** (-2.0 * jnp.arange(half_size, dtype=jnp.float32) / head_size)
    angles = positions.astype(jnp.float32)[:, None] * frequencies[None, :]
    cosine = jnp.cos(angles)
    sine_part = jnp.sin(angles)
    cosine_lookup = jnp.concatenate([cosine, cosine], axis=1)[:, None, :]
    sine_lookup = jnp.concatenate([sine_part, sine_part], axis=1)[:, None, :]
    return (cosine_lookup, sine_lookup)


def apply_rotary(head_rows, cosine_lookup, sine_lookup):
    half_size = head_rows.shape[-1] // 2
    turned = jnp.concatenate([-head_rows[..., half_size:], head_rows[..., :half_size]], axis=-1)
    return head_rows * cosine_lookup + turned * sine_lookup


def inverse_rotary(grad_rows, cosine_lookup, sine_lookup):
    half_size = grad_rows.shape[-1] // 2
    moved = grad_rows * sine_lookup
    turned_back = jnp.concatenate([moved[..., half_size:], -moved[..., :half_size]], axis=-1)
    return grad_rows * cosine_lookup + turned_back


def gather_columns(shards):
    return (
        lax.all_gather(shards[0], "ctx", axis=1, tiled=True),
        lax.all_gather(shards[1], "ctx", axis=1, tiled=True),
        lax.all_gather(shards[2], "ctx", axis=1, tiled=True),
        lax.all_gather(shards[3], "ctx", axis=1, tiled=True),
        lax.all_gather(shards[4], "ctx", axis=1, tiled=True),
        lax.all_gather(shards[5], "ctx", axis=1, tiled=True),
        lax.all_gather(shards[6], "ctx", axis=1, tiled=True),
    )


def gather_rows(shards):
    return (
        lax.all_gather(shards[0], "fsdp", axis=0, tiled=True),
        lax.all_gather(shards[1], "fsdp", axis=0, tiled=True),
        lax.all_gather(shards[2], "fsdp", axis=0, tiled=True),
        lax.all_gather(shards[3], "fsdp", axis=0, tiled=True),
        lax.all_gather(shards[4], "fsdp", axis=0, tiled=True),
        lax.all_gather(shards[5], "fsdp", axis=0, tiled=True),
        lax.all_gather(shards[6], "fsdp", axis=0, tiled=True),
    )


def reduce_columns(terms):
    return (
        lax.psum_scatter(
            terms[0].astype(jnp.bfloat16), "ctx", scatter_dimension=1, tiled=True
        ).astype(jnp.float32),
        lax.psum_scatter(
            terms[1].astype(jnp.bfloat16), "ctx", scatter_dimension=1, tiled=True
        ).astype(jnp.float32),
        lax.psum_scatter(
            terms[2].astype(jnp.bfloat16), "ctx", scatter_dimension=1, tiled=True
        ).astype(jnp.float32),
        lax.psum_scatter(
            terms[3].astype(jnp.bfloat16), "ctx", scatter_dimension=1, tiled=True
        ).astype(jnp.float32),
        lax.psum_scatter(
            terms[4].astype(jnp.bfloat16), "ctx", scatter_dimension=1, tiled=True
        ).astype(jnp.float32),
        lax.psum_scatter(
            terms[5].astype(jnp.bfloat16), "ctx", scatter_dimension=1, tiled=True
        ).astype(jnp.float32),
        lax.psum_scatter(
            terms[6].astype(jnp.bfloat16), "ctx", scatter_dimension=1, tiled=True
        ).astype(jnp.float32),
    )


def reduce_rows(terms):
    return (
        lax.psum_scatter(
            terms[0].astype(jnp.bfloat16), "fsdp", scatter_dimension=0, tiled=True
        ).astype(jnp.float32),
        lax.psum_scatter(
            terms[1].astype(jnp.bfloat16), "fsdp", scatter_dimension=0, tiled=True
        ).astype(jnp.float32),
        lax.psum_scatter(
            terms[2].astype(jnp.bfloat16), "fsdp", scatter_dimension=0, tiled=True
        ).astype(jnp.float32),
        lax.psum_scatter(
            terms[3].astype(jnp.bfloat16), "fsdp", scatter_dimension=0, tiled=True
        ).astype(jnp.float32),
        lax.psum_scatter(
            terms[4].astype(jnp.bfloat16), "fsdp", scatter_dimension=0, tiled=True
        ).astype(jnp.float32),
        lax.psum_scatter(
            terms[5].astype(jnp.bfloat16), "fsdp", scatter_dimension=0, tiled=True
        ).astype(jnp.float32),
        lax.psum_scatter(
            terms[6].astype(jnp.bfloat16), "fsdp", scatter_dimension=0, tiled=True
        ).astype(jnp.float32),
    )


def attend_piece(
    state_carry, query_head_split, query_pos, key_row_block, value_row_block, key_pos, scale_factor
):
    running_top, running_total, running_sum = state_carry
    rows_per_piece = key_row_block.shape[0]
    key_head_split = key_row_block.reshape(rows_per_piece, KEY_VALUE_HEADS, HEAD_WIDTH)
    value_head_split = value_row_block.reshape(rows_per_piece, KEY_VALUE_HEADS, HEAD_WIDTH)
    scores = (
        jnp.einsum(
            "oufm,aum->ufoa", query_head_split, key_head_split, preferred_element_type=jnp.float32
        )
        * scale_factor
    )
    visible = key_pos[None, :] <= query_pos[:, None]
    masked = jnp.where(visible, scores, MASK_FLOOR)
    new_top = jnp.maximum(running_top, jnp.max(masked, axis=-1))
    factor = jnp.exp(running_top - new_top)
    weights = jnp.where(visible, jnp.exp(masked - new_top[..., None]), 0.0)
    new_total = running_total * factor + jnp.sum(weights, axis=-1)
    new_sum = running_sum * factor[..., None] + jnp.einsum(
        "sjwx,xsr->sjwr",
        weights.astype(jnp.bfloat16),
        value_head_split,
        preferred_element_type=jnp.float32,
    )
    return (new_top, new_total, new_sum)


def backward_piece(
    grad_query,
    query_head_split,
    query_pos,
    key_row_block,
    value_row_block,
    key_pos,
    log_total,
    head_gradient,
    delta_rows,
    scale_factor,
):
    rows_per_piece = key_row_block.shape[0]
    key_head_split = key_row_block.reshape(rows_per_piece, KEY_VALUE_HEADS, HEAD_WIDTH)
    value_head_split = value_row_block.reshape(rows_per_piece, KEY_VALUE_HEADS, HEAD_WIDTH)
    scores = (
        jnp.einsum(
            "oufm,aum->ufoa", query_head_split, key_head_split, preferred_element_type=jnp.float32
        )
        * scale_factor
    )
    visible = key_pos[None, :] <= query_pos[:, None]
    masked = jnp.where(visible, scores, MASK_FLOOR)
    probabilities = jnp.where(visible, jnp.exp(masked - log_total[..., None]), 0.0)
    value_gradient = jnp.einsum(
        "jsvi,vjsr->ijr",
        probabilities.astype(jnp.bfloat16),
        head_gradient,
        preferred_element_type=jnp.float32,
    )
    grad_probs = jnp.einsum(
        "oufm,aum->ufoa", head_gradient, value_head_split, preferred_element_type=jnp.float32
    )
    score_gradient = (probabilities * (grad_probs - delta_rows[..., None]) * scale_factor).astype(
        jnp.bfloat16
    )
    updated = grad_query + jnp.einsum(
        "fuhc,cfl->hful", score_gradient, key_head_split, preferred_element_type=jnp.float32
    )
    key_gradient = jnp.einsum(
        "jsvi,vjsr->ijr", score_gradient, query_head_split, preferred_element_type=jnp.float32
    )
    return (
        updated,
        key_gradient.reshape(rows_per_piece, KEY_VALUE_HEADS * HEAD_WIDTH),
        value_gradient.reshape(rows_per_piece, KEY_VALUE_HEADS * HEAD_WIDTH),
    )


def over_blocks(state_carry, step_function, key_row_block, value_row_block, key_pos):
    rows_per_piece = key_row_block.shape[0]
    rows_per_block = math.gcd(rows_per_piece, 512)
    block_count = rows_per_piece // rows_per_block

    def over_advance(inner_state, block_set):
        return (step_function(inner_state, block_set[0], block_set[1], block_set[2]), None)

    block_sets = (
        key_row_block.reshape(block_count, rows_per_block, key_row_block.shape[1]),
        value_row_block.reshape(block_count, rows_per_block, value_row_block.shape[1]),
        key_pos.reshape(block_count, rows_per_block),
    )
    final_state, unused = lax.scan(over_advance, state_carry, block_sets)
    return final_state


def backward_blocks(grad_query, step_function, key_row_block, value_row_block, key_pos):
    rows_per_piece = key_row_block.shape[0]
    rows_per_block = math.gcd(rows_per_piece, 512)
    block_count = rows_per_piece // rows_per_block

    def backward_advance(inner_query, block_set):
        updated, key_gradient, value_gradient = step_function(
            inner_query, block_set[0], block_set[1], block_set[2]
        )
        return (updated, (key_gradient, value_gradient))

    block_sets = (
        key_row_block.reshape(block_count, rows_per_block, key_row_block.shape[1]),
        value_row_block.reshape(block_count, rows_per_block, value_row_block.shape[1]),
        key_pos.reshape(block_count, rows_per_block),
    )
    final_query, stacked = lax.scan(backward_advance, grad_query, block_sets)
    return (
        final_query,
        stacked[0].reshape(rows_per_piece, -1),
        stacked[1].reshape(rows_per_piece, -1),
    )


def body(
    tokens,
    pair_table,
    gain_attn,
    w_query,
    w_key,
    w_value,
    w_out,
    gain_mlp,
    w_gate,
    w_up,
    w_down,
    cotangent,
):
    ctx_count = lax.axis_size("ctx")
    ctx_index = lax.axis_index("ctx")
    device_rows = tokens.shape[1]
    query_per_group = QUERY_HEADS // KEY_VALUE_HEADS
    scale_factor = 1.0 / math.sqrt(HEAD_WIDTH)
    all_pos = token_positions(pair_table, device_rows, ctx_count)
    own_pos = lax.dynamic_slice_in_dim(all_pos, ctx_index * device_rows, device_rows)
    cosine_lookup, sine_lookup = rope_tables(own_pos, HEAD_WIDTH)
    shards = (w_query, w_key, w_value, w_out, w_gate, w_up, w_down)
    full_weights = gather_rows(gather_columns(shards))
    query_w, key_w, value_w, out_w, gate_w, up_w, down_w = full_weights
    inputs = tokens[0].astype(jnp.float32)
    inverse_one = lax.rsqrt(jnp.mean(inputs * inputs, axis=-1, keepdims=True) + EPSILON)
    normed_one = inputs * inverse_one
    rounded_one = (normed_one * gain_attn).astype(jnp.bfloat16)
    query_raw = jnp.dot(rounded_one, query_w, preferred_element_type=jnp.float32).reshape(
        device_rows, QUERY_HEADS, HEAD_WIDTH
    )
    unrotated_key = jnp.dot(rounded_one, key_w, preferred_element_type=jnp.float32).reshape(
        device_rows, KEY_VALUE_HEADS, HEAD_WIDTH
    )
    value_local = jnp.dot(rounded_one, value_w, preferred_element_type=jnp.float32).astype(
        jnp.bfloat16
    )
    query_head_split = (
        apply_rotary(query_raw, cosine_lookup, sine_lookup)
        .astype(jnp.bfloat16)
        .reshape(device_rows, KEY_VALUE_HEADS, query_per_group, HEAD_WIDTH)
    )
    key_local = (
        apply_rotary(unrotated_key, cosine_lookup, sine_lookup)
        .astype(jnp.bfloat16)
        .reshape(device_rows, KEY_VALUE_HEADS * HEAD_WIDTH)
    )

    def forward_step(state_carry, key_row_block, value_row_block, key_pos):
        return attend_piece(
            state_carry,
            query_head_split,
            own_pos,
            key_row_block,
            value_row_block,
            key_pos,
            scale_factor,
        )

    initial = (
        jnp.full((KEY_VALUE_HEADS, query_per_group, device_rows), MASK_FLOOR, jnp.float32),
        jnp.zeros((KEY_VALUE_HEADS, query_per_group, device_rows), jnp.float32),
        jnp.zeros((KEY_VALUE_HEADS, query_per_group, device_rows, HEAD_WIDTH), jnp.float32),
    )
    gathered = (
        lax.all_gather(key_local, "ctx", axis=0, tiled=True),
        lax.all_gather(value_local, "ctx", axis=0, tiled=True),
    )
    final_state = over_blocks(initial, forward_step, gathered[0], gathered[1], all_pos)
    running_top, running_total, running_sum = final_state
    mixture = (running_sum / running_total[..., None]).transpose(2, 0, 1, 3)
    log_total = running_top + jnp.log(running_total)
    attended = mixture.reshape(device_rows, QUERY_HEADS * HEAD_WIDTH).astype(jnp.bfloat16)
    middle = inputs + jnp.dot(attended, out_w, preferred_element_type=jnp.float32)
    inverse_two = lax.rsqrt(jnp.mean(middle * middle, axis=-1, keepdims=True) + EPSILON)
    normed_two = middle * inverse_two
    rounded_two = (normed_two * gain_mlp).astype(jnp.bfloat16)
    gate_values = jnp.dot(rounded_two, gate_w, preferred_element_type=jnp.float32)
    up_values = jnp.dot(rounded_two, up_w, preferred_element_type=jnp.float32)
    sigmoid_gate = jax.nn.sigmoid(gate_values)
    silu_gate = gate_values * sigmoid_gate
    hidden_units = (silu_gate * up_values).astype(jnp.bfloat16)
    result = (middle + jnp.dot(hidden_units, down_w, preferred_element_type=jnp.float32)).astype(
        jnp.bfloat16
    )
    grad_result = cotangent[0]
    grad_down = jnp.einsum(
        "tf,td->fd", hidden_units, grad_result, preferred_element_type=jnp.float32
    )
    grad_hidden = jnp.einsum("td,fd->tf", grad_result, down_w, preferred_element_type=jnp.float32)
    grad_gate_values = (
        grad_hidden * up_values * sigmoid_gate * (1.0 + gate_values * (1.0 - sigmoid_gate))
    ).astype(jnp.bfloat16)
    grad_up_values = (grad_hidden * silu_gate).astype(jnp.bfloat16)
    grad_gate = jnp.einsum(
        "td,tf->df", rounded_two, grad_gate_values, preferred_element_type=jnp.float32
    )
    grad_up = jnp.einsum(
        "td,tf->df", rounded_two, grad_up_values, preferred_element_type=jnp.float32
    )
    grad_normed_two = jnp.einsum(
        "tf,df->td", grad_gate_values, gate_w, preferred_element_type=jnp.float32
    ) + jnp.einsum("tf,df->td", grad_up_values, up_w, preferred_element_type=jnp.float32)
    grad_gain_mlp = jnp.sum(grad_normed_two * normed_two, axis=0)
    scaled_two = grad_normed_two * gain_mlp
    grad_middle = grad_result.astype(jnp.float32) + inverse_two * (
        scaled_two - normed_two * jnp.mean(scaled_two * normed_two, axis=-1, keepdims=True)
    )
    grad_branch = grad_middle.astype(jnp.bfloat16)
    grad_out_w = jnp.einsum("td,te->de", attended, grad_branch, preferred_element_type=jnp.float32)
    attended_gradient = jnp.einsum(
        "te,de->td", grad_branch, out_w, preferred_element_type=jnp.float32
    ).astype(jnp.bfloat16)
    head_gradient = attended_gradient.reshape(
        device_rows, KEY_VALUE_HEADS, query_per_group, HEAD_WIDTH
    )
    delta_rows = jnp.sum(head_gradient.astype(jnp.float32) * mixture, axis=-1).transpose(1, 2, 0)
    key_all, value_all = gathered

    def backward_step(grad_query, key_row_block, value_row_block, key_pos):
        return backward_piece(
            grad_query,
            query_head_split,
            own_pos,
            key_row_block,
            value_row_block,
            key_pos,
            log_total,
            head_gradient,
            delta_rows,
            scale_factor,
        )

    empty_query_gradient = jnp.zeros(
        (device_rows, KEY_VALUE_HEADS, query_per_group, HEAD_WIDTH), jnp.float32
    )
    grad_query_turned, grad_key_all, grad_value_all = backward_blocks(
        empty_query_gradient, backward_step, key_all, value_all, all_pos
    )
    rotated_key_gradient, grad_value_local = (
        lax.psum_scatter(
            grad_key_all.astype(jnp.bfloat16), "ctx", scatter_dimension=0, tiled=True
        ).astype(jnp.float32),
        lax.psum_scatter(
            grad_value_all.astype(jnp.bfloat16), "ctx", scatter_dimension=0, tiled=True
        ).astype(jnp.float32),
    )
    grad_query_rows = (
        inverse_rotary(
            grad_query_turned.reshape(device_rows, QUERY_HEADS, HEAD_WIDTH),
            cosine_lookup,
            sine_lookup,
        )
        .reshape(device_rows, QUERY_HEADS * HEAD_WIDTH)
        .astype(jnp.bfloat16)
    )
    grad_key_rows = (
        inverse_rotary(
            rotated_key_gradient.reshape(device_rows, KEY_VALUE_HEADS, HEAD_WIDTH),
            cosine_lookup,
            sine_lookup,
        )
        .reshape(device_rows, KEY_VALUE_HEADS * HEAD_WIDTH)
        .astype(jnp.bfloat16)
    )
    grad_value_rows = grad_value_local.astype(jnp.bfloat16)
    grad_query_w = jnp.einsum(
        "td,te->de", rounded_one, grad_query_rows, preferred_element_type=jnp.float32
    )
    grad_key_w = jnp.einsum(
        "td,te->de", rounded_one, grad_key_rows, preferred_element_type=jnp.float32
    )
    grad_value_w = jnp.einsum(
        "td,te->de", rounded_one, grad_value_rows, preferred_element_type=jnp.float32
    )
    grad_normed_one = jnp.einsum(
        "te,de->td", grad_query_rows, query_w, preferred_element_type=jnp.float32
    )
    grad_normed_one = grad_normed_one + jnp.einsum(
        "te,de->td", grad_key_rows, key_w, preferred_element_type=jnp.float32
    )
    grad_normed_one = grad_normed_one + jnp.einsum(
        "te,de->td", grad_value_rows, value_w, preferred_element_type=jnp.float32
    )
    grad_gain_attn = jnp.sum(grad_normed_one * normed_one, axis=0)
    scaled_one = grad_normed_one * gain_attn
    grad_inputs = grad_middle + inverse_one * (
        scaled_one - normed_one * jnp.mean(scaled_one * normed_one, axis=-1, keepdims=True)
    )
    weight_terms = (
        grad_query_w,
        grad_key_w,
        grad_value_w,
        grad_out_w,
        grad_gate,
        grad_up,
        grad_down,
    )
    reduced = reduce_columns(reduce_rows(weight_terms))
    gain_totals = lax.psum((grad_gain_attn, grad_gain_mlp), ("ctx", "fsdp"))
    return (
        result[None],
        grad_inputs[None],
        gain_totals[0],
        reduced[0],
        reduced[1],
        reduced[2],
        reduced[3],
        gain_totals[1],
        reduced[4],
        reduced[5],
        reduced[6],
    )


def solution(mesh):
    placed = (
        P("fsdp", "ctx", None),
        P(),
        P(),
        P("fsdp", "ctx"),
        P("fsdp", "ctx"),
        P("fsdp", "ctx"),
        P("fsdp", "ctx"),
        P(),
        P("fsdp", "ctx"),
        P("fsdp", "ctx"),
        P("fsdp", "ctx"),
        P("fsdp", "ctx", None),
    )
    return jax.shard_map(
        body,
        mesh=mesh,
        in_specs=placed,
        out_specs=(
            P("fsdp", "ctx", None),
            P("fsdp", "ctx", None),
            P(),
            P("fsdp", "ctx"),
            P("fsdp", "ctx"),
            P("fsdp", "ctx"),
            P("fsdp", "ctx"),
            P(),
            P("fsdp", "ctx"),
            P("fsdp", "ctx"),
            P("fsdp", "ctx"),
        ),
        check_vma=False,
    )
```

profile of v0, /device:TPU:0, one launch (start us, length us, event | category | flops | bytes accessed | tf_op | source)
XLA Modules:
  0.0 2332.0 jit_solution(2842509313176013519)
XLA Ops:
  9.5 86.0 %all-gather.2 = bf16[32,30,240]{2,1,0:T(8,128)(2,1)S(1)} all-gather(bf16[1,30,240]{2,1,0:T(8,128)(2,1)} %bitcast.356), channel_id=1, replica_groups=mesh['ctx'=32,'fsdp'=4] {'ctx'}, dimensions={0}, use_global_device_ids=true | all-gather | bytes 475200 | tf_op jit(solution)/shard_map/all_gather | solution.py:58
  96.8 76.6 %all-gather = bf16[32,10,240]{2,1,0:T(8,128)(2,1)S(1)} all-gather(bf16[1,10,240]{2,1,0:T(8,128)(2,1)S(1)} %bitcast.359), channel_id=1, replica_groups=mesh['ctx'=32,'fsdp'=4] {'ctx'}, dimensions={0}, use_global_device_ids=true | all-gather | bytes 158400 | tf_op jit(solution)/shard_map/all_gather | solution.py:59
  173.5 9.4 all-gather.1
  186.3 78.8 %all-gather.3 = bf16[32,10,240]{2,1,0:T(8,128)(2,1)S(1)} all-gather(bf16[1,10,240]{2,1,0:T(8,128)(2,1)S(1)} %bitcast.360), channel_id=1, replica_groups=mesh['ctx'=32,'fsdp'=4] {'ctx'}, dimensions={0}, use_global_device_ids=true | all-gather | bytes 158400 | tf_op jit(solution)/shard_map/all_gather | solution.py:60
  265.2 9.5 all-gather.4
  277.0 78.6 %all-gather.5 = bf16[32,30,240]{2,1,0:T(8,128)(2,1)S(1)} all-gather(bf16[1,30,240]{2,1,0:T(8,128)(2,1)S(1)} %bitcast.357), channel_id=1, replica_groups=mesh['ctx'=32,'fsdp'=4] {'ctx'}, dimensions={0}, use_global_device_ids=true | all-gather | bytes 475200 | tf_op jit(solution)/shard_map/all_gather | solution.py:61
  362.6 108.9 %all-gather.36.cloned.1.call-done = bf16[32,30,640]{2,1,0:T(8,128)(2,1)} async-done(((bf16[1,30,640]{2,1,0:T(8,128)(2,1)}), bf16[32,30,640]{2,1,0:T(8,128)(2,1)}) %all-gather.36.cloned.1.call-update) | async-done | bytes 1228816 | tf_op jit(solution)/shard_map/all_gather | solution.py:64
  474.1 25.3 %all-gather.20.cloned.1.call-done = bf16[960,960]{1,0:T(8,128)(2,1)} async-done(((bf16[240,960]{1,0:T(8,128)(2,1)}), bf16[960,960]{1,0:T(8,128)(2,1)}) %all-gather.20.cloned.1.call-update) | async-done | bytes 1843216 | tf_op jit(solution)/shard_map/all_gather | solution.py:70
  503.2 125.1 %all-gather.18.cloned.1.call-done = bf16[4096,320]{0,1:T(8,128)(2,1)} async-done(((bf16[128,320]{0,1:T(8,128)(2,1)}), bf16[4096,320]{0,1:T(8,128)(2,1)}) %all-gather.18.cloned.1.call-update) | async-done | bytes 2621456 | tf_op jit(solution)/shard_map/all_gather | solution.py:316
  631.9 126.0 %all-gather.22.cloned.1.call-done = bf16[4096,320]{0,1:T(8,128)(2,1)} async-done(((bf16[128,320]{0,1:T(8,128)(2,1)}), bf16[4096,320]{0,1:T(8,128)(2,1)}) %all-gather.22.cloned.1.call-update) | async-done | bytes 2621456 | tf_op jit(solution)/shard_map/all_gather | solution.py:317
  761.4 79.7 %while.30 = (s32[]{:T(128)}, f32[5,3,128]{2,1,0:T(4,128)S(1)}, f32[5,3,128]{2,1,0:T(4,128)S(1)}, f32[5,3,128,64]{2,3,1,0:T(8,128)S(1)}, s32[8,512]{1,0:T(8,128)}...) while((s32[]{:T(128)}, f32[5,3,128]{2,1,0:T(4,128)S(1)}, ...), condition=%wide.region_5.6_spmd.clone, body=%wide.region_2.5_spmd.clone.sunk | while | flops 264881536 | bytes 31111844 | solution.py:222
  849.2 23.7 %all-gather.32.cloned.1.call-done = bf16[960,2560]{1,0:T(8,128)(2,1)} async-done(((bf16[240,2560]{1,0:T(8,128)(2,1)}), bf16[960,2560]{1,0:T(8,128)(2,1)}) %all-gather.32.cloned.1.call-update) | async-done | bytes 4915216 | tf_op jit(solution)/shard_map/all_gather | solution.py:75
  877.3 39.2 %all-gather.34.cloned.1.call-done = bf16[2560,960]{0,1:T(8,128)(2,1)} async-done(((bf16[640,960]{0,1:T(8,128)(2,1)}), bf16[2560,960]{0,1:T(8,128)(2,1)}) %all-gather.34.cloned.1.call-update) | async-done | bytes 4915216 | tf_op jit(solution)/shard_map/all_gather | solution.py:76
  916.5 5.5 multiply_convert_fusion
  931.8 103.4 %while.31 = (s32[]{:T(128)}, f32[128,5,3,64]{0,3,2,1:T(8,128)S(1)}, bf16[8,512,320]{1,2,0:T(8,128)(2,1)}, bf16[8,512,320]{1,2,0:T(8,128)(2,1)}, bf16[8,512,320]{...) while((s32[]{:T(128)}, f32[128,5,3,64]{0,3,2,1:T(8,128)S(1)}, ...), condition=%wide.region_10.11_spmd.clone, body=%wide.region_9.10_spmd.clone.sunk | while | flops 642236416 | bytes 40492364 | solution.py:242
  1039.8 4.6 copy.157
  1044.4 161.1 %reduce-scatter.38.cloned.1.call-done = bf16[128,320]{1,0:T(8,128)(2,1)} async-done(((bf16[4096,320]{1,0:T(8,128)(2,1)}), bf16[128,320]{1,0:T(8,128)(2,1)}) %reduce-scatter.38.cloned.1.call-update) | async-done | bytes 81936
  1208.3 161.3 %reduce-scatter.40.cloned.1.call-done = bf16[128,320]{1,0:T(8,128)(2,1)} async-done(((bf16[4096,320]{1,0:T(8,128)(2,1)}), bf16[128,320]{1,0:T(8,128)(2,1)}) %reduce-scatter.40.cloned.1.call-update) | async-done | bytes 81936
  1385.1 12.8 reduce-scatter.42.cloned.1.call-done
  1399.6 30.3 %reduce-scatter.44.cloned.1.call-done = bf16[240,320]{1,0:T(8,128)(2,1)} async-done(((bf16[960,320]{1,0:T(8,128)(2,1)}), bf16[240,320]{1,0:T(8,128)(2,1)}) %reduce-scatter.44.cloned.1.call-update) | async-done | bytes 153616
  1431.6 37.8 %reduce-scatter.30.cloned.1.call-done = bf16[240,960]{1,0:T(8,128)(2,1)} async-done(((bf16[960,960]{1,0:T(8,128)(2,1)}), bf16[240,960]{1,0:T(8,128)(2,1)}) %reduce-scatter.30.cloned.1.call-update) | async-done | bytes 460816 | tf_op jit(solution)/shard_map/reduce_scatter | solution.py:108
  1469.5 39.7 %reduce-scatter.32.cloned.1.call-done = bf16[240,960]{1,0:T(8,128)(2,1)} async-done(((bf16[960,960]{1,0:T(8,128)(2,1)}), bf16[240,960]{1,0:T(8,128)(2,1)}) %reduce-scatter.32.cloned.1.call-update) | async-done | bytes 460816 | tf_op jit(solution)/shard_map/reduce_scatter | solution.py:117
  1512.9 8.1 copy.154
  1521.2 46.1 %reduce-scatter.34.cloned.1.call-done = bf16[240,2560]{1,0:T(8,128)(2,1)} async-done(((bf16[960,2560]{1,0:T(8,128)(2,1)}), bf16[240,2560]{1,0:T(8,128)(2,1)}) %reduce-scatter.34.cloned.1.call-update) | async-done | bytes 1228816 | tf_op jit(solution)/shard_map/reduce_scatter | solution.py:120
  1572.5 4.6 fusion.31
  1578.8 46.8 %reduce-scatter.36.cloned.1.call-done = bf16[240,2560]{1,0:T(8,128)(2,1)} async-done(((bf16[960,2560]{1,0:T(8,128)(2,1)}), bf16[240,2560]{1,0:T(8,128)(2,1)}) %reduce-scatter.36.cloned.1.call-update) | async-done | bytes 1228816 | tf_op jit(solution)/shard_map/reduce_scatter | solution.py:123
  1630.6 66.6 %all-reduce.6 = (f32[960]{0:T(1024)}, f32[960]{0:T(1024)}) all-reduce(f32[960]{0:T(1024)S(1)} %get-tuple-element.393, f32[960]{0:T(1024)S(1)} %copy-done.40), channel_id=1, replica_groups=mesh['ctx'=32,'fsdp'=4] {'ctx','fsdp'}, use_global_device_ids=true, to_apply=%region_15.16 | all-reduce | flops 1920 | bytes 15360 | tf_op jit(solution)/shard_map/psum | solution.py:450
  1699.2 239.3 %all-reduce.10.cloned.1.call-done = (bf16[240,960]{1,0:T(8,128)(2,1)}, bf16[240,320]{0,1:T(8,128)(2,1)}, bf16[240,320]{0,1:T(8,128)(2,1)}, bf16[240,960]{1,0:T(8,128)(2,1)}) async-done(((bf16[240,960]{1,0:T(8,128)(2,1)}, bf16[240,320]{0,1:T(8,128)(2,1)}, bf16[240,320]{0,1:T(8,128)(2,1)}, bf16[240,960]{1,0:T(8,128)(2,1)}), (bf16[240,960]{1,0:T(8,128)(2,1)}, bf16[240,320]{0,1:T(8,128)(2,1)}, ...) | async-done | bytes 1228816
  1941.9 57.7 %reduce-scatter.50.cloned.1.call-done = bf16[640,960]{1,0:T(8,128)(2,1)} async-done(((bf16[2560,960]{1,0:T(8,128)(2,1)}), bf16[640,960]{1,0:T(8,128)(2,1)}) %reduce-scatter.50.cloned.1.call-update) | async-done | bytes 1228816
  2001.7 90.7 %fusion = bf16[640,32]{0,1:T(8,128)(2,1)S(1)} fusion(bf16[640,960]{0,1:T(8,128)(2,1)S(1)} %copy.155), kind=kCustom, calls=%all-reduce-scatter | all-reduce-scatter fusion | flops 655361 | bytes 1270272
  2099.3 63.9 %reduce-scatter.46.cloned.1.call-done = bf16[80,240]{1,0:T(8,128)(2,1)} async-done(((bf16[2560,240]{1,0:T(8,128)(2,1)}), bf16[80,240]{1,0:T(8,128)(2,1)}) %reduce-scatter.46.cloned.1.call-update) | async-done | bytes 38416
  2164.9 158.2 %reduce-scatter.48.cloned.1.call-done = bf16[80,240]{1,0:T(8,128)(2,1)} async-done(((bf16[2560,240]{1,0:T(8,128)(2,1)}), bf16[80,240]{1,0:T(8,128)(2,1)}) %reduce-scatter.48.cloned.1.call-update) | async-done | bytes 38416
  (502 shorter events, 290.6 us)
Async XLA Ops:
  7.2 349.6 %all-gather.26.cloned.1.call-start = ((), (), s32[]{:S(2)}) async-start(), calls=%async_computation.15 | async-start | bytes 1351680 | tf_op jit(solution)/shard_map/all_gather | solution.py:62
  7.9 351.5 %all-gather.30.cloned.1.call-start = ((), (), s32[]{:S(2)}) async-start(), calls=%async_computation.17 | async-start | bytes 1351680 | tf_op jit(solution)/shard_map/all_gather | solution.py:63
  8.7 462.9 %all-gather.36.cloned.1.call-start = ((), (), s32[]{:S(2)}) async-start(), calls=%async_computation.24 | async-start | bytes 1351680 | tf_op jit(solution)/shard_map/all_gather | solution.py:64
  9.4 490.0 %all-gather.20.cloned.1.call-start = ((), (), s32[]{:S(2)}) async-start(), calls=%async_computation.12 | async-start | bytes 2457600 | tf_op jit(solution)/shard_map/all_gather | solution.py:70
  96.7 531.7 %all-gather.18.cloned.1.call-start = ((), (), s32[]{:S(2)}) async-start(), calls=%async_computation.11 | async-start | bytes 2703360 | tf_op jit(solution)/shard_map/all_gather | solution.py:316
  184.9 318.2 %copy-start.25 = (f32[128,64]{0,1:T(8,128)}, f32[128,64]{0,1:T(8,128)S(1)}, u32[]{:S(2)}) copy-start(f32[128,64]{0,1:T(8,128)S(1)} %pad_maximum_fusion.3) | copy-start | bytes 98308
  185.1 317.2 %copy-start.37 = (f32[128]{0:T(128)}, f32[128]{0:T(128)S(1)}, u32[]{:S(2)}) copy-start(f32[128]{0:T(128)S(1)} %add_rsqrt_fusion.1) | copy-start | bytes 1540
  186.3 571.6 %all-gather.22.cloned.1.call-start = ((), (), s32[]{:S(2)}) async-start(), calls=%async_computation.13 | async-start | bytes 2703360 | tf_op jit(solution)/shard_map/all_gather | solution.py:317
  276.9 564.2 %all-gather.24.cloned.1.call-start = ((), (), s32[]{:S(2)}) async-start(), calls=%async_computation.14 | async-start | bytes 2457600 | tf_op jit(solution)/shard_map/all_gather | solution.py:73
  356.8 488.1 %all-gather.28.cloned.1.call-start = ((), (), s32[]{:S(2)}) async-start(), calls=%async_computation.16 | async-start | bytes 6144000 | tf_op jit(solution)/shard_map/all_gather | solution.py:74
  359.3 513.6 %all-gather.32.cloned.1.call-start = ((), (), s32[]{:S(2)}) async-start(), calls=%async_computation.18 | async-start | bytes 6144000 | tf_op jit(solution)/shard_map/all_gather | solution.py:75
  361.9 554.6 %all-gather.34.cloned.1.call-start = ((), (), s32[]{:S(2)}) async-start(), calls=%async_computation.19 | async-start | bytes 6144000 | tf_op jit(solution)/shard_map/all_gather | solution.py:76
  473.9 731.6 %reduce-scatter.38.cloned.1.call-start = ((), (), s32[]{:S(2)}) async-start(), calls=%async_computation.25 | async-start | bytes 3244032
  1039.7 329.9 %reduce-scatter.40.cloned.1.call-start = ((), (), s32[]{:S(2)}) async-start(), calls=%async_computation.26 | async-start | bytes 3244032
  1039.8 166.7 %copy-start.26 = (f32[128,64]{0,1:T(8,128)S(1)}, f32[128,64]{0,1:T(8,128)}, u32[]{:S(2)}) copy-start(f32[128,64]{0,1:T(8,128)} %copy-done.25) | copy-start | bytes 98308
  1044.3 162.3 %copy-start.33 = (f32[960]{0:T(1024)S(1)}, f32[960]{0:T(1024)}, u32[]{:S(2)}) copy-start(f32[960]{0:T(1024)} %param.18) | copy-start | bytes 11524
  1044.3 162.3 %copy-start.38 = (f32[128]{0:T(128)S(1)}, f32[128]{0:T(128)}, u32[]{:S(2)}) copy-start(f32[128]{0:T(128)} %copy-done.37) | copy-start | bytes 1540
  1044.4 353.5 %reduce-scatter.42.cloned.1.call-start = ((), (), s32[]{:S(2)}) async-start(), calls=%async_computation.27 | async-start | bytes 921600
  1206.6 165.7 %copy-start.27 = (bf16[128,320]{0,1:T(8,128)(2,1)}, bf16[128,320]{0,1:T(8,128)(2,1)S(1)}, u32[]{:S(2)}) copy-start(bf16[128,320]{0,1:T(8,128)(2,1)S(1)} %fusion.64) | copy-start | bytes 245764
  1208.3 221.6 %reduce-scatter.44.cloned.1.call-start = ((), (), s32[]{:S(2)}) async-start(), calls=%async_computation.28 | async-start | bytes 921600
  1372.2 97.2 %reduce-scatter.30.cloned.1.call-start = ((), (), s32[]{:S(2)}) async-start(), calls=%async_computation.20 | async-start | bytes 2457600 | tf_op jit(solution)/shard_map/reduce_scatter | solution.py:108
  1374.6 134.6 %reduce-scatter.32.cloned.1.call-start = ((), (), s32[]{:S(2)}) async-start(), calls=%async_computation.21 | async-start | bytes 2457600 | tf_op jit(solution)/shard_map/reduce_scatter | solution.py:117
  1376.7 190.6 %reduce-scatter.34.cloned.1.call-start = ((), (), s32[]{:S(2)}) async-start(), calls=%async_computation.22 | async-start | bytes 6144000 | tf_op jit(solution)/shard_map/reduce_scatter | solution.py:120
  1380.3 245.3 %reduce-scatter.36.cloned.1.call-start = ((), (), s32[]{:S(2)}) async-start(), calls=%async_computation.23 | async-start | bytes 6144000 | tf_op jit(solution)/shard_map/reduce_scatter | solution.py:123
  1385.0 124.2 %copy-start.12 = (bf16[128,2560]{1,0:T(8,128)(2,1)S(1)}, bf16[128,2560]{1,0:T(8,128)(2,1)}, u32[]{:S(2)}) copy-start(bf16[128,2560]{1,0:T(8,128)(2,1)} %get-tuple-element.455) | copy-start | bytes 1966084
  1385.0 124.2 %copy-start.22 = (bf16[1,128,960]{1,2,0:T(8,128)(2,1)S(1)}, bf16[1,128,960]{1,2,0:T(8,128)(2,1)}, u32[]{:S(2)}) copy-start(bf16[1,128,960]{1,2,0:T(8,128)(2,1)} %param.27) | copy-start | bytes 737284
  1385.1 553.5 %all-reduce.10.cloned.1.call-start = ((), (), s32[]{:S(2)}) async-start(), calls=%async_computation.32 | async-start | bytes 2621440
  1509.2 490.3 %reduce-scatter.50.cloned.1.call-start = ((), (), s32[]{:S(2)}) async-start(), calls=%async_computation.31 | async-start | bytes 6553600
  1521.1 642.1 %reduce-scatter.46.cloned.1.call-start = ((), (), s32[]{:S(2)}) async-start(), calls=%async_computation.29 | async-start | bytes 1351680
  1569.7 753.3 %reduce-scatter.48.cloned.1.call-start = ((), (), s32[]{:S(2)}) async-start(), calls=%async_computation.30 | async-start | bytes 1351680
  2092.4 5.8 collective-permute-start
  2094.2 4.0 collective-permute-start.1
  (92 other events, 1243.4 us)
Sparse Core Ops, SparseCore 0:
  9.7 154.4 all-gather.25
  165.8 152.1 all-gather.29
  319.6 151.8 all-gather.35
  473.6 25.7 all-gather.19
  501.4 126.8 all-gather.17
  630.4 127.4 all-gather.21
  759.5 25.8 all-gather.23
  787.1 42.0 all-gather.27
  830.9 42.0 all-gather.31
  874.5 41.9 all-gather.33
  1039.8 165.6 reduce-scatter.37
  1207.9 161.7 reduce-scatter.39
  1372.3 25.5 reduce-scatter.41
  1400.6 29.2 reduce-scatter.43
  1432.4 36.9 reduce-scatter.29
  1472.2 36.9 reduce-scatter.31
  1511.7 55.5 reduce-scatter.33
  1570.0 55.5 reduce-scatter.35
  1628.3 310.2 all-reduce.9
  1941.3 58.2 reduce-scatter.49
  2001.9 161.2 reduce-scatter.45
  2165.7 157.3 reduce-scatter.47
where the time goes:
time: 2340 us; the launch traced here: 2330 us
  waiting for transfers between devices  1510 us (65%)
  blocking collectives  496 us (21%)
  matrix products  145 us (6%)
  local copies, waits for them, and re-layouts  110 us (5%)
  other arithmetic  51.9 us (2%)
    unnamed x32, waiting for transfers between devices  887 us
    all_gather x1, waiting for transfers between devices, body(): lax.all_gather(value_local, 'ctx', axis=0, tiled=True)  126 us
    all_gather x1, waiting for transfers between devices, body(): lax.all_gather(key_local, 'ctx', axis=0, tiled=True)  125 us
    all_gather x1, waiting for transfers between devices, gather_columns(): lax.all_gather(shards[6], 'ctx', axis=1, tiled=True)  109 us
    unnamed x1, blocking collectives  90.7 us
    all_gather x1, blocking collectives, gather_columns(): lax.all_gather(shards[0], 'ctx', axis=1, tiled=True)  86 us
    all_gather x1, blocking collectives, gather_columns(): lax.all_gather(shards[2], 'ctx', axis=1, tiled=True)  78.8 us
    all_gather x1, blocking collectives, gather_columns(): lax.all_gather(shards[3], 'ctx', axis=1, tiled=True)  78.6 us
  transfers between devices with their start and end apart: 24, of which 18 were waited for; matrix products, arithmetic and copies ran while one was open for 12% of the time, Pallas kernels for 0%

commit v1 on v0

v1 whole, which is shorter than its diff:
```python
import functools
import math

import jax
import jax.numpy as jnp
from jax import lax
from jax.experimental import pallas as pl
from jax.experimental.pallas import tpu as pltpu
from jax.sharding import PartitionSpec as P

QUERY_HEADS = 15
KEY_VALUE_HEADS = 5
HEAD_WIDTH = 64


EPSILON = 1e-05
THETA = 10000.0
MASK_FLOOR = -1e30


def rope_tables(positions, head_size):
    half_size = head_size // 2
    frequencies = THETA ** (-2.0 * jnp.arange(half_size, dtype=jnp.float32) / head_size)
    angles = positions.astype(jnp.float32)[:, None] * frequencies[None, :]
    cosine = jnp.cos(angles)
    sine_part = jnp.sin(angles)
    cosine_lookup = jnp.concatenate([cosine, cosine], axis=1)[:, None, :]
    sine_lookup = jnp.concatenate([sine_part, sine_part], axis=1)[:, None, :]
    return (cosine_lookup, sine_lookup)


def apply_rotary(head_rows, cosine_lookup, sine_lookup):
    half_size = head_rows.shape[-1] // 2
    turned = jnp.concatenate([-head_rows[..., half_size:], head_rows[..., :half_size]], axis=-1)
    return head_rows * cosine_lookup + turned * sine_lookup


def inverse_rotary(grad_rows, cosine_lookup, sine_lookup):
    half_size = grad_rows.shape[-1] // 2
    moved = grad_rows * sine_lookup
    turned_back = jnp.concatenate([moved[..., half_size:], -moved[..., :half_size]], axis=-1)
    return grad_rows * cosine_lookup + turned_back


AXES = ("y", "xl", "z", "xh", "core")
CTX = ("y", "xl", "z")
FSDP = ("xh", "core")


def shift(block, axis, step):
    size = lax.axis_size(axis)
    return lax.ppermute(block, axis, [(i, (i + step) % size) for i in range(size)])


def ring_gather(block, axis, halves=None):
    ahead = shift(block, axis, -1)
    behind = shift(block, axis, 1)
    if halves is None:
        return block, ahead, shift(block, axis, 2), behind
    split, join = halves
    across = join(shift(split(ahead)[0], axis, -1), shift(split(behind)[1], axis, 1))
    return block, ahead, across, behind


def ring_scatter(terms, axis, halves=None):
    own, ahead, across, behind = terms
    if halves is None:
        arrived = (
            shift(ahead, axis, 1),
            shift(behind, axis, -1),
            shift(across, axis, 2),
        )
    else:
        split, join = halves
        first, second = split(across)
        first = shift(first, axis, 1)
        second = shift(second, axis, -1)
        ahead_first, ahead_second = split(ahead)
        behind_first, behind_second = split(behind)
        arrived = (
            shift(join(add(ahead_first, first), ahead_second), axis, 1),
            shift(join(behind_first, add(behind_second, second)), axis, -1),
        )
    return add(own, *arrived)


def add(*terms):
    total = terms[0].astype(jnp.float32)
    for term in terms[1:]:
        total = total + term.astype(jnp.float32)
    return total.astype(jnp.bfloat16)


def leading_halves():
    return (lambda block: (block[:1], block[1:])), (
        lambda first, second: jnp.concatenate([first, second], axis=0)
    )


def row_halves():
    def split(block):
        half = block.shape[0] // 2
        return block[:half], block[half:]

    return split, (lambda first, second: jnp.concatenate([first, second], axis=0))


def place(blocks, axis, dim):
    index = lax.axis_index(axis)
    shape = blocks[0].shape
    whole = jnp.zeros(shape[:dim] + (4,) + shape[dim:], blocks[0].dtype)
    for j, block in enumerate(blocks):
        whole = lax.dynamic_update_index_in_dim(whole, block, (index + j) % 4, dim)
    return whole


def pick(whole, axis, dim):
    index = lax.axis_index(axis)
    return [
        lax.dynamic_index_in_dim(whole, (index + j) % 4, dim, keepdims=False) for j in range(4)
    ]


def pair_gather(block, axis, dim, stack=True):
    other = shift(block, axis, 1)
    first = lax.axis_index(axis) == 0
    low = jnp.where(first, block, other)
    high = jnp.where(first, other, block)
    if stack:
        return jnp.stack([low, high], axis=dim)
    return jnp.concatenate([low, high], axis=dim)


def pair_scatter(low, high, axis):
    first = lax.axis_index(axis) == 0
    keep = jnp.where(first, low, high)
    away = jnp.where(first, high, low)
    return add(keep, shift(away, axis, 1))


def gather_y_last(block):
    pair, rows, width = block.shape
    block = place(ring_gather(block, "z"), "z", 1)
    block = pair_gather(block, "xl", 1).reshape(pair, 8 * rows, width)
    block = place(ring_gather(block, "y", leading_halves()), "y", 1)
    return block.reshape(pair, 32 * rows, width)


def scatter_y_first(block):
    pair, rows, width = block.shape
    rows = rows // 32
    block = block.reshape(pair, 4, 8 * rows, width)
    block = ring_scatter(pick(block, "y", 1), "y", leading_halves())
    block = block.reshape(pair, 2, 4, rows, width)
    block = pair_scatter(block[:, 0], block[:, 1], "xl")
    return ring_scatter(pick(block, "z", 1), "z")


def gather_z_last(block):
    pair, rows, width = block.shape
    block = pair_gather(block, "xl", 1)
    block = place(ring_gather(block, "y"), "y", 1)
    block = place(ring_gather(block, "z", leading_halves()), "z", 3)
    return block.reshape(pair, 32 * rows, width)


def scatter_z_first(block):
    pair, rows, width = block.shape
    rows = rows // 32
    block = block.reshape(pair, 4, 2, 4, rows, width)
    block = ring_scatter(pick(block, "z", 3), "z", leading_halves())
    block = ring_scatter(pick(block, "y", 1), "y")
    return pair_scatter(block[:, 0], block[:, 1], "xl")


def gather_keys(block, near, far):
    other = shift(block, "xl", 1)
    block = jnp.concatenate([block, other], axis=0)
    block = jnp.concatenate(ring_gather(block, near), axis=0)
    return jnp.concatenate(ring_gather(block, far, row_halves()), axis=0)


def scatter_keys(block, near, far):
    block = ring_scatter(jnp.split(block, 4, axis=0), far, row_halves())
    block = ring_scatter(jnp.split(block, 4, axis=0), near)
    own, other = jnp.split(block, 2, axis=0)
    return add(own, shift(other, "xl", 1))


def total_sum(block):
    for axis in ("core", "xh", "xl"):
        block = block + shift(block, axis, 1)
    for axis in ("z", "y"):
        block = (block + shift(block, axis, 2)) + (shift(block, axis, 1) + shift(block, axis, -1))
    return block


def block_table(pair_table):
    y, xl, z = (lax.axis_index(axis) for axis in CTX)
    four = jnp.arange(4, dtype=jnp.int32)
    ys = ((y + four) % 4) * 8
    zs = (z + four) % 4
    xs = ((xl + jnp.arange(2, dtype=jnp.int32)) % 2) * 4
    low = ys[:, None, None] + zs[None, :, None] + xs[None, None, :]
    high = ys[None, :, None] + zs[:, None, None] + xs[None, None, :]
    count = pair_table.shape[0]

    def paired(owners):
        matches = owners.reshape(-1)[:, None] == jnp.arange(count, dtype=jnp.int32)[None, :]
        return jnp.sum(jnp.where(matches, pair_table[None, :], 0), axis=1, dtype=jnp.int32)

    return jnp.concatenate([paired(low), 2 * count - 1 - paired(high)])


def half_columns(rows, width):
    core = lax.axis_index("core")
    parts = [rows[:, i * width : (i + 1) * width] for i in range(4)]
    even = jnp.concatenate([parts[0], parts[2]], axis=1)
    odd = jnp.concatenate([parts[1], parts[3]], axis=1)
    return jnp.where(core == 0, even, odd), jnp.where(core == 0, odd, even)


def both(rows, weights):
    return jnp.einsum(
        "td,ed->te", rows[0], weights[0], preferred_element_type=jnp.float32
    ) + jnp.einsum("td,ed->te", rows[1], weights[1], preferred_element_type=jnp.float32)


def back_through(grads, weights):
    own = jnp.einsum("te,ed->td", grads, weights[0], preferred_element_type=jnp.float32)
    other = jnp.einsum("te,ed->td", grads, weights[1], preferred_element_type=jnp.float32)
    return merge_columns(own, other)


def merge_columns(own, other):
    core = lax.axis_index("core")
    even = jnp.where(core == 0, own, other)
    odd = jnp.where(core == 0, other, own)
    width = own.shape[1] // 2
    return jnp.concatenate(
        [even[:, :width], odd[:, :width], even[:, width:], odd[:, width:]], axis=1
    )


def weight_term(left, right):
    return jnp.einsum("te,td->ed", left, right, preferred_element_type=jnp.float32).astype(
        jnp.bfloat16
    )


TILE = 512
LANES = 2 * HEAD_WIDTH


def lane_pair(part):
    return slice(part // 2 * LANES, part // 2 * LANES + LANES)


def fill_bias(base_ref, query_ref, bias_ref, half_rows):
    def step(chunk, carry):
        rows = pl.ds(chunk * half_rows, half_rows)
        position = base_ref[chunk] + lax.broadcasted_iota(jnp.int32, (half_rows, LANES), 0)
        bias_ref[rows, :] = jnp.where(position <= query_ref[...], 0.0, MASK_FLOOR)
        return carry

    lax.fori_loop(0, base_ref.shape[0], step, 0)


def tile_scores(kv_ref, rows, q_ref, bias, group):
    scores = lax.dot_general(
        kv_ref[rows, lane_pair(group)],
        q_ref[group],
        (((1,), (1,)), ((), ())),
        preferred_element_type=jnp.float32,
    )
    return scores + bias


def attend_kernel(base_ref, query_ref, kv_ref, q_ref, o_ref, lse_ref, bias_ref, *, half_rows):
    fill_bias(base_ref, query_ref, bias_ref, half_rows)
    wide = q_ref.shape[1]
    tiles = kv_ref.shape[0] // TILE
    for group in range(KEY_VALUE_HEADS):

        def step(tile, carry, group=group):
            top, total, mixed = carry
            rows = pl.ds(pl.multiple_of(tile * TILE, TILE), TILE)
            bias = jnp.concatenate([bias_ref[rows, :]] * (wide // LANES), axis=1)
            scores = tile_scores(kv_ref, rows, q_ref, bias, group)
            new_top = jnp.maximum(top, jnp.max(scores, axis=0, keepdims=True))
            factor = jnp.exp(top - new_top)
            weights = jnp.exp(scores - new_top)
            total = total * factor + jnp.sum(weights, axis=0, keepdims=True)
            mixed = mixed * factor + lax.dot_general(
                kv_ref[rows, lane_pair(KEY_VALUE_HEADS + group)],
                weights.astype(jnp.bfloat16),
                (((0,), (0,)), ((), ())),
                preferred_element_type=jnp.float32,
            )
            return new_top, total, mixed

        top, total, mixed = lax.fori_loop(
            0,
            tiles,
            step,
            (
                jnp.full((1, wide), MASK_FLOOR, jnp.float32),
                jnp.zeros((1, wide), jnp.float32),
                jnp.zeros((LANES, wide), jnp.float32),
            ),
        )
        side = (KEY_VALUE_HEADS + group) % 2 * HEAD_WIDTH
        o_ref[group] = (mixed / total)[side : side + HEAD_WIDTH]
        lse_ref[group] = top + jnp.log(total)


def backward_kernel(
    base_ref,
    query_ref,
    kv_ref,
    q_ref,
    do_ref,
    lse_ref,
    delta_ref,
    dkv_ref,
    dq_ref,
    bias_ref,
    *,
    half_rows,
):
    fill_bias(base_ref, query_ref, bias_ref, half_rows)
    wide = q_ref.shape[1]
    tiles = kv_ref.shape[0] // TILE
    dq_ref[...] = jnp.zeros_like(dq_ref)

    def step(tile, carry):
        rows = pl.ds(pl.multiple_of(tile * TILE, TILE), TILE)
        bias = jnp.concatenate([bias_ref[rows, :]] * (wide // LANES), axis=1)
        sums = [None] * KEY_VALUE_HEADS

        def collect(part, term):
            pair = part // 2
            sums[pair] = term if sums[pair] is None else sums[pair] + term

        for group in range(KEY_VALUE_HEADS):
            scores = tile_scores(kv_ref, rows, q_ref, bias, group)
            probs = jnp.exp(scores - lse_ref[group])
            grad_probs = lax.dot_general(
                kv_ref[rows, lane_pair(KEY_VALUE_HEADS + group)],
                do_ref[group],
                (((1,), (1,)), ((), ())),
                preferred_element_type=jnp.float32,
            )
            ds = (probs * (grad_probs - delta_ref[group])).astype(jnp.bfloat16)
            collect(
                KEY_VALUE_HEADS + group,
                jnp.dot(
                    probs.astype(jnp.bfloat16), do_ref[group], preferred_element_type=jnp.float32
                ),
            )
            collect(group, jnp.dot(ds, q_ref[group], preferred_element_type=jnp.float32))
            dq_ref[group] += lax.dot_general(
                kv_ref[rows, lane_pair(group)],
                ds,
                (((0,), (0,)), ((), ())),
                preferred_element_type=jnp.float32,
            )
        for pair in range(KEY_VALUE_HEADS):
            dkv_ref[rows, pair * LANES : (pair + 1) * LANES] = sums[pair].astype(jnp.bfloat16)
        return carry

    lax.fori_loop(0, tiles, step, 0)


def in_vmem():
    return pl.BlockSpec(memory_space=pltpu.VMEM)


def in_smem():
    return pl.BlockSpec(memory_space=pltpu.SMEM)


def spread_heads(rows, offset):
    count = rows.shape[0]
    heads = rows.reshape(count, KEY_VALUE_HEADS, -1, HEAD_WIDTH).transpose(1, 2, 0, 3)
    heads = heads.reshape(KEY_VALUE_HEADS, -1, HEAD_WIDTH)
    blank = jnp.zeros_like(heads)
    left = jnp.concatenate([heads, blank], axis=2)
    right = jnp.concatenate([blank, heads], axis=2)
    side = (offset + jnp.arange(KEY_VALUE_HEADS, dtype=jnp.int32)) % 2
    return jnp.where(side[:, None, None] == 0, left, right)


def join_heads(heads, count):
    heads = heads.reshape(KEY_VALUE_HEADS, HEAD_WIDTH, -1, count)
    return heads.transpose(3, 0, 2, 1).reshape(count, QUERY_HEADS * HEAD_WIDTH)


def attend(bases, query_pos, key_value, queries, half_rows):
    groups, wide, lanes = queries.shape
    keys = key_value.shape[0]
    return pl.pallas_call(
        functools.partial(attend_kernel, half_rows=half_rows),
        out_shape=(
            jax.ShapeDtypeStruct((groups, HEAD_WIDTH, wide), jnp.float32),
            jax.ShapeDtypeStruct((groups, 1, wide), jnp.float32),
        ),
        in_specs=[in_smem(), in_vmem(), in_vmem(), in_vmem()],
        out_specs=(in_vmem(), in_vmem()),
        scratch_shapes=[pltpu.VMEM((keys, lanes), jnp.float32)],
        compiler_params=pltpu.CompilerParams(vmem_limit_bytes=40 * 2**20),
        cost_estimate=pl.CostEstimate(
            flops=4 * groups * wide * lanes * keys,
            bytes_accessed=keys * 640 * 2,
            transcendentals=groups * wide * keys,
        ),
        name="attend",
    )(bases, query_pos, key_value, queries)


def attend_backward(bases, query_pos, key_value, queries, head_grads, lse, delta, half_rows):
    groups, wide, lanes = queries.shape
    keys = key_value.shape[0]
    return pl.pallas_call(
        functools.partial(backward_kernel, half_rows=half_rows),
        out_shape=(
            jax.ShapeDtypeStruct(key_value.shape, jnp.bfloat16),
            jax.ShapeDtypeStruct((groups, lanes, wide), jnp.float32),
        ),
        in_specs=[in_smem()] + [in_vmem()] * 6,
        out_specs=(in_vmem(), in_vmem()),
        scratch_shapes=[pltpu.VMEM((keys, lanes), jnp.float32)],
        compiler_params=pltpu.CompilerParams(vmem_limit_bytes=40 * 2**20),
        cost_estimate=pl.CostEstimate(
            flops=10 * groups * wide * lanes * keys,
            bytes_accessed=keys * 640 * 4,
            transcendentals=groups * wide * keys,
        ),
        name="attend_backward",
    )(bases, query_pos, key_value, queries, head_grads, lse, delta)


def body(
    tokens,
    pair_table,
    gain_attn,
    w_query,
    w_key,
    w_value,
    w_out,
    gain_mlp,
    w_gate,
    w_up,
    w_down,
    cotangent,
):
    device_rows = tokens.shape[1]
    half_rows = device_rows // 2
    width = HEAD_WIDTH * KEY_VALUE_HEADS
    query_per_group = QUERY_HEADS // KEY_VALUE_HEADS
    scale_factor = 1.0 / math.sqrt(HEAD_WIDTH)
    within = jnp.arange(half_rows, dtype=jnp.int32)
    blocks = block_table(pair_table)
    all_pos = (blocks[:, None] * half_rows + within[None, :]).reshape(-1)
    chunk_count = blocks.shape[0]
    own_pos = jnp.concatenate(
        [blocks[0] * half_rows + within, blocks[chunk_count // 2] * half_rows + within]
    )
    cosine_lookup, sine_lookup = rope_tables(own_pos, HEAD_WIDTH)

    def gather_halves(shards, gather):
        packed = jnp.stack([shard.T for shard in shards], axis=0)
        packed = pair_gather(packed, "xh", 2, stack=False)
        own = gather(packed)
        return own, shift(own, "core", 1)

    key_value_w = gather_halves((w_key, w_value), gather_y_last)
    query_out_w = gather_halves((w_query, w_out), gather_y_last)
    gate_up_w = gather_halves((w_gate, w_up), gather_z_last)
    down_own = gather_y_last(pair_gather(w_down.T, "xh", 0))
    down_w = (down_own, shift(down_own, "core", 1))
    rows_w = w_query.shape[0]
    ff_w = w_down.shape[0]

    inputs = tokens[0].astype(jnp.float32)
    inverse_one = lax.rsqrt(jnp.mean(inputs * inputs, axis=-1, keepdims=True) + EPSILON)
    normed_one = inputs * inverse_one
    rounded_one = half_columns((normed_one * gain_attn).astype(jnp.bfloat16), rows_w)
    unrotated_key = both(rounded_one, [half[0] for half in key_value_w]).reshape(
        device_rows, KEY_VALUE_HEADS, HEAD_WIDTH
    )
    value_local = both(rounded_one, [half[1] for half in key_value_w]).astype(jnp.bfloat16)
    key_local = (
        apply_rotary(unrotated_key, cosine_lookup, sine_lookup)
        .astype(jnp.bfloat16)
        .reshape(device_rows, width)
    )
    key_value = jnp.concatenate([key_local, value_local], axis=1)
    key_value_all = jnp.concatenate(
        [
            gather_keys(key_value[:half_rows], "z", "y"),
            gather_keys(key_value[half_rows:], "y", "z"),
        ],
        axis=0,
    )
    query_raw = both(rounded_one, [half[0] for half in query_out_w]).reshape(
        device_rows, QUERY_HEADS, HEAD_WIDTH
    )
    query_heads = apply_rotary(query_raw, cosine_lookup, sine_lookup).astype(jnp.bfloat16)
    queries = spread_heads(
        query_heads.reshape(device_rows, QUERY_HEADS * HEAD_WIDTH)
        * jnp.asarray(scale_factor, jnp.bfloat16),
        0,
    )
    bases = blocks * half_rows
    query_pos = own_pos[None, :]
    mixed, log_total = attend(bases, query_pos, key_value_all, queries, half_rows)
    mixture = join_heads(mixed, device_rows)
    attended = mixture.astype(jnp.bfloat16)
    out_rows = [half[1] for half in query_out_w]
    middle = inputs + both(half_columns(attended, rows_w), out_rows)
    inverse_two = lax.rsqrt(jnp.mean(middle * middle, axis=-1, keepdims=True) + EPSILON)
    normed_two = middle * inverse_two
    rounded_two = half_columns((normed_two * gain_mlp).astype(jnp.bfloat16), rows_w)
    gate_values = both(rounded_two, [half[0] for half in gate_up_w])
    up_values = both(rounded_two, [half[1] for half in gate_up_w])
    sigmoid_gate = jax.nn.sigmoid(gate_values)
    silu_gate = gate_values * sigmoid_gate
    hidden_units = half_columns((silu_gate * up_values).astype(jnp.bfloat16), ff_w)
    result = middle
    for hidden_half, down_half in zip(hidden_units, down_w):
        for i in range(2):
            result = result + jnp.einsum(
                "tf,df->td",
                hidden_half[:, i * ff_w : (i + 1) * ff_w],
                down_half[i],
                preferred_element_type=jnp.float32,
            )
    result = result.astype(jnp.bfloat16)
    grad_result = cotangent[0]
    down_terms = [
        jnp.stack(
            [weight_term(grad_result, half[:, :ff_w]), weight_term(grad_result, half[:, ff_w:])]
        )
        for half in hidden_units
    ]
    grad_down = add(down_terms[0], shift(down_terms[1], "core", 1))
    grad_down = scatter_y_first(grad_down)
    grad_down = pair_scatter(grad_down[0], grad_down[1], "xh")
    grad_hidden = merge_columns(
        *[
            jnp.concatenate(
                [
                    jnp.einsum("td,df->tf", grad_result, half[i], preferred_element_type=jnp.float32)
                    for i in range(2)
                ],
                axis=1,
            )
            for half in down_w
        ]
    )
    grad_gate_values = (
        grad_hidden * up_values * sigmoid_gate * (1.0 + gate_values * (1.0 - sigmoid_gate))
    ).astype(jnp.bfloat16)
    grad_up_values = (grad_hidden * silu_gate).astype(jnp.bfloat16)

    def scatter_halves(lefts, rights, scatter):
        terms = [
            jnp.stack([weight_term(left, half) for left, half in zip(lefts, halves)])
            for halves in rights
        ]
        term = scatter(add(terms[0], shift(terms[1], "core", 1)))
        return pair_scatter(term[..., :rows_w], term[..., rows_w:], "xh")

    grad_gate_up = scatter_halves(
        (grad_gate_values, grad_up_values), [(half, half) for half in rounded_two], scatter_z_first
    )
    grad_normed_two = back_through(grad_gate_values, [half[0] for half in gate_up_w])
    grad_normed_two = grad_normed_two + back_through(
        grad_up_values, [half[1] for half in gate_up_w]
    )
    grad_gain_mlp = jnp.sum(grad_normed_two * normed_two, axis=0)
    scaled_two = grad_normed_two * gain_mlp
    grad_middle = grad_result.astype(jnp.float32) + inverse_two * (
        scaled_two - normed_two * jnp.mean(scaled_two * normed_two, axis=-1, keepdims=True)
    )
    grad_branch = grad_middle.astype(jnp.bfloat16)
    attended_gradient = back_through(grad_branch, out_rows).astype(jnp.bfloat16)
    delta_rows = jnp.sum(
        (attended_gradient.astype(jnp.float32) * mixture).reshape(
            device_rows, KEY_VALUE_HEADS, query_per_group, HEAD_WIDTH
        ),
        axis=-1,
    )
    delta_rows = delta_rows.transpose(1, 2, 0).reshape(KEY_VALUE_HEADS, 1, -1)
    key_value_terms, grad_query_lanes = attend_backward(
        bases,
        query_pos,
        key_value_all,
        queries,
        spread_heads(attended_gradient, KEY_VALUE_HEADS),
        log_total,
        delta_rows,
        half_rows,
    )
    grad_query_turned = (
        join_heads(
            jnp.stack(
                [
                    grad_query_lanes[g, g % 2 * HEAD_WIDTH : (g % 2 + 1) * HEAD_WIDTH]
                    for g in range(KEY_VALUE_HEADS)
                ]
            ),
            device_rows,
        )
        * scale_factor
    )
    key_value_gradient = jnp.concatenate(
        [
            scatter_keys(key_value_terms[: chunk_count // 2 * half_rows], "z", "y"),
            scatter_keys(key_value_terms[chunk_count // 2 * half_rows :], "y", "z"),
        ],
        axis=0,
    )
    grad_query_rows = (
        inverse_rotary(
            grad_query_turned.reshape(device_rows, QUERY_HEADS, HEAD_WIDTH),
            cosine_lookup,
            sine_lookup,
        )
        .reshape(device_rows, QUERY_HEADS * HEAD_WIDTH)
        .astype(jnp.bfloat16)
    )
    grad_query_out = scatter_halves(
        (grad_query_rows, grad_branch),
        list(zip(rounded_one, half_columns(attended, rows_w))),
        scatter_y_first,
    )
    grad_key_rows = (
        inverse_rotary(
            key_value_gradient[:, :width]
            .astype(jnp.float32)
            .reshape(device_rows, KEY_VALUE_HEADS, HEAD_WIDTH),
            cosine_lookup,
            sine_lookup,
        )
        .reshape(device_rows, width)
        .astype(jnp.bfloat16)
    )
    grad_value_rows = key_value_gradient[:, width:]
    grad_key_value = scatter_halves(
        (grad_key_rows, grad_value_rows), [(half, half) for half in rounded_one], scatter_y_first
    )
    grad_normed_one = back_through(grad_query_rows, [half[0] for half in query_out_w])
    grad_normed_one = grad_normed_one + back_through(
        grad_key_rows, [half[0] for half in key_value_w]
    )
    grad_normed_one = grad_normed_one + back_through(
        grad_value_rows, [half[1] for half in key_value_w]
    )
    grad_gain_attn = jnp.sum(grad_normed_one * normed_one, axis=0)
    scaled_one = grad_normed_one * gain_attn
    grad_inputs = grad_middle + inverse_one * (
        scaled_one - normed_one * jnp.mean(scaled_one * normed_one, axis=-1, keepdims=True)
    )

    def out(term):
        return term.astype(jnp.float32).T

    return (
        result[None],
        grad_inputs[None],
        total_sum(grad_gain_attn),
        out(grad_query_out[0]),
        out(grad_key_value[0]),
        out(grad_key_value[1]),
        out(grad_query_out[1]),
        total_sum(grad_gain_mlp),
        out(grad_gate_up[0]),
        out(grad_gate_up[1]),
        out(grad_down),
    )


def solution(mesh):
    grid = mesh.devices.reshape(4, 2, 4, 2, 2)
    fine = jax.sharding.Mesh(grid, AXES)
    rows = P(FSDP, CTX, None)
    weight = P(FSDP, CTX)
    return jax.shard_map(
        body,
        mesh=fine,
        in_specs=(
            rows,
            P(),
            P(),
            weight,
            weight,
            weight,
            weight,
            P(),
            weight,
            weight,
            weight,
            rows,
        ),
        out_specs=(
            rows,
            rows,
            P(),
            weight,
            weight,
            weight,
            weight,
            P(),
            weight,
            weight,
            weight,
        ),
        check_vma=False,
    )
```

time: 2340 us -> 590 us (0.25)
  waiting for transfers between devices: 1510 us -> 154 us
  blocking collectives: 496 us -> 0 us
  starting transfers between devices: 4.09 us -> 164 us
  matrix products: 145 us -> 55.7 us
  Pallas kernels: 0 us -> 49.6 us
    unnamed x32 -> x0, waiting for transfers between devices: 887 us -> none
    all_gather x10 -> x0, waiting for transfers between devices: 448 us -> none  [the longest x1 126 us: body(): lax.all_gather(value_local, 'ctx', axis=0, tiled=True)]
    all_gather x6 -> x0, blocking collectives: 339 us -> none  [the longest x1 86 us: gather_columns(): lax.all_gather(shards[0], 'ctx', axis=1, tiled=True)]
    reduce_scatter x4 -> x0, waiting for transfers between devices: 170 us -> none  [the longest x1 46.8 us: reduce_rows(): lax.psum_scatter(terms[5].astype(jnp.bfloat16), 'fsdp', scatter_dimension...]
    ppermute x0 -> x130, starting transfers between devices: none -> 164 us  [shift(): lax.ppermute(block, axis, [(i, (i + step) % size) for i in range(size)])]
    ppermute x0 -> x130, waiting for transfers between devices: none -> 154 us  [shift(): lax.ppermute(block, axis, [(i, (i + step) % size) for i in range(size)])]
    unnamed x1 -> x0, blocking collectives: 90.7 us -> none
    dot_general x77 -> x48, matrix products: 145 us -> 55.7 us  [the longest x16 14.6 us: weight_term(): jnp.einsum('te,td->ed', left, right, preferred_element_type=jnp.float32)]
  transfers between devices with their start and end apart: 24 -> 130, of which waited for: 18 -> 51; matrix products, arithmetic and copies ran while one was open for 12% -> 29% of each run, Pallas kernels for 0% -> 4%
where the time goes in v1:
time: 590 us; the launch traced here: 580 us
  starting transfers between devices  164 us (28%)
  waiting for transfers between devices  154 us (26%)
  local copies, waits for them, and re-layouts  93.9 us (16%)
  other arithmetic  58.3 us (10%)
  matrix products  55.7 us (9%)
  Pallas kernels  49.6 us (8%)
    ppermute x130, starting transfers between devices, shift(): lax.ppermute(block, axis, [(i, (i + step) % size) for i in range(size)])  164 us
    ppermute x130, waiting for transfers between devices, shift(): lax.ppermute(block, axis, [(i, (i + step) % size) for i in range(size)])  154 us
    pallas_call x1, Pallas kernels, attend(): pl.pallas_call(functools.partial(attend_kernel, half_rows=half_rows), out...  25.8 us
    pallas_call x1, Pallas kernels, attend_backward(): pl.pallas_call(functools.partial(backward_kernel, half_rows=half_rows), o...  23.8 us
    dynamic_update_slice x30, local copies, waits for them, and re-layouts, place(): whole = lax.dynamic_update_index_in_dim(whole, block, (index + j) % 4, dim)  18 us
    unnamed x180, local copies, waits for them, and re-layouts  16.1 us
    dot_general x16, matrix products, weight_term(): jnp.einsum('te,td->ed', left, right, preferred_element_type=jnp.float32)  14.6 us
    convert_element_type x29, other arithmetic, add(): return total.astype(jnp.bfloat16)  14.5 us
  transfers between devices with their start and end apart: 130, of which 51 were waited for; matrix products, arithmetic and copies ran while one was open for 29% of the time, Pallas kernels for 4%

profile of v1, /device:TPU:0, one launch (start us, length us, event | category | flops | bytes accessed | tf_op | source)
XLA Modules:
  0.0 579.9 jit_solution(7957160463206255637)
XLA Ops:
  17.1 4.1 collective-permute-start.1
  23.0 3.4 collective-permute-start.27
  42.1 3.3 collective-permute-start.38
  47.4 5.0 collective-permute-done.7
  59.6 4.8 collective-permute-done.8
  93.0 3.4 collective-permute-start.32
  103.0 5.5 collective-permute-done.34
  142.8 6.4 %collective-permute-done.14 = bf16[512,640]{1,0:T(8,128)(2,1)S(1)} collective-permute-done((bf16[512,640]{1,0:T(8,128)(2,1)S(1)}, bf16[512,640]{1,0:T(8,128)(2,1)S(1)}, u32[]{:S(2)}, u32[]{:S(2)}) %collective-permute-start.14) | collective-permute-done | bytes 655392 | tf_op jit(solution)/shard_map/ppermute | solution.py:52
  155.3 5.0 collective-permute-done.43
  160.5 4.7 collective-permute-done.15
  170.7 5.6 collective-permute-done.21
  184.1 7.7 %copy.345 = bf16[2,2560,480]{1,2,0:T(8,128)(2,1)} copy(bf16[2,2560,480]{2,1,0:T(8,128)(2,1)} %bitcast.75) | data formatting | bytes 9830400 | tf_op jit(solution)/shard_map/reshape | solution.py:164
  191.8 5.4 fusion.142
  199.0 3.7 collective-permute-start.23
  220.0 25.8 %attend.1 = (f32[5,64,384]{2,1,0:T(8,128)S(1)}, f32[5,1,384]{2,1,0:T(1,128)S(1)}) custom-call(s32[64]{0:T(128)S(1)} %add_multiply_fusion.base_ref, s32[1,128]{1,0:T(1,128)S(1)} %get-tuple-element.232.query_ref, bf16[4096,640]{1,0:T(8,128)(2,1)S(1)} %copy-done.1, bf16[5,384,128]{2,1,0:T(8,128)(2,1)S(1)} %pad_select_fusion.1.q_ref), custom_call_target="tpu_custom_call" | custom-call | flops 4026531840 | bytes 5242880 | tf_op jit(solution)/shard_map/attend/pallas_call | solution.py:402
  283.0 23.8 %attend_backward.1 = (bf16[4096,640]{1,0:T(8,128)(2,1)S(1)}, f32[5,128,384]{2,1,0:T(8,128)S(1)}) custom-call(s32[64]{0:T(128)S(1)} %add_multiply_fusion.base_ref, s32[1,128]{1,0:T(1,128)S(1)} %get-tuple-element.232.query_ref, bf16[4096,640]{1,0:T(8,128)(2,1)S(1)} %copy-done.2, bf16[5,384,128]{2,1,0:T(8,128)(2,1)S(1)} %pad_select_fusion.1.q_ref, ...), custom_call_target="tpu_custom_call" | custom-call | flops 10066329600 | bytes 10485760 | tf_op jit(solution)/shard_map/attend_backward/pallas_call | solution.py:424
  314.3 3.5 collective-permute-start.58
  354.5 11.4 %collective-permute-done.108 = f32[960]{0:T(1024)S(1)} collective-permute-done((f32[960]{0:T(1024)S(1)}, f32[960]{0:T(1024)S(1)}, u32[]{:S(2)}, u32[]{:S(2)}) %collective-permute-start.108) | collective-permute-done | bytes 3872 | tf_op jit(solution)/shard_map/ppermute | solution.py:52
  370.0 4.7 collective-permute-done.107
  379.0 6.1 %collective-permute-done.70 = bf16[128,640]{1,0:T(8,128)(2,1)S(1)} collective-permute-done((bf16[128,640]{1,0:T(8,128)(2,1)S(1)}, bf16[128,640]{1,0:T(8,128)(2,1)S(1)}, u32[]{:S(2)}, u32[]{:S(2)}) %collective-permute-start.70) | collective-permute-done | bytes 163872 | tf_op jit(solution)/shard_map/ppermute | solution.py:52
  389.6 3.4 collective-permute-done.62
  429.0 3.4 collective-permute-done.75
  458.4 3.4 collective-permute-start.80
  490.1 3.7 collective-permute-start.124
  494.8 6.0 %add_convert_fusion = bf16[2,2560,480]{1,2,0:T(8,128)(2,1)} fusion(bf16[2,2560,480]{1,2,0:T(8,128)(2,1)} %collective-permute-done.110, bf16[1,2560,480]{1,2,0:T(8,128)(2,1)S(1)} %copy-done.9, bf16[1,2560,480]{1,2,0:T(8,128)(2,1)S(1)} %copy-done.10), kind=kLoop, calls=%fused_computation | loop fusion | flops 12288000 | bytes 14745600 | tf_op jit(solution)/shard_map/convert_element_type | solution.py:91
  500.8 7.9 %copy.370 = bf16[2,2560,480]{2,1,0:T(8,128)(2,1)} copy(bf16[2,2560,480]{1,2,0:T(8,128)(2,1)} %add_convert_fusion) | data formatting | bytes 9830400 | tf_op jit(solution)/shard_map/convert_element_type | solution.py:91
  517.4 11.9 %collective-permute-done.111 = bf16[1,4,2,80,480]{4,3,2,1,0:T(8,128)(2,1)S(1)} collective-permute-done((bf16[1,4,2,80,480]{4,3,2,1,0:T(8,128)(2,1)S(1)}, bf16[1,4,2,80,480]{4,3,2,1,0:T(8,128)(2,1)S(1)}, u32[]{:S(2)}, u32[]{:S(2)}) %collective-permute-start.111) | collective-permute-done | bytes 614432 | tf_op jit(solution)/shard_map/ppermute | solution.py:52
  529.9 3.4 collective-permute-start.114
  538.4 4.6 collective-permute-done.125
  548.5 4.9 collective-permute-done.112
  559.1 3.7 collective-permute-done.117
  562.9 4.1 collective-permute-done.116
  (711 shorter events, 372.6 us)
Async XLA Ops:
  0.7 27.7 %collective-permute-start.46 = (bf16[30,640]{1,0:T(8,128)(2,1)}, bf16[30,640]{1,0:T(8,128)(2,1)S(1)}, u32[]{:S(2)}, u32[]{:S(2)}) collective-permute-start(bf16[30,640]{1,0:T(8,128)(2,1)} %bitcast.686), channel_id=1, source_target_pairs={{0,2},{2,0},{1,3},{3,1},{4,6},{6,4},{5,7},{7,5},{8,10},{10,8},{9,1... | collective-permute-start | bytes 115208 | tf_op jit(solution)/shard_map/ppermute | solution.py:52
  9.9 20.4 %collective-permute-start.36 = (bf16[2,80,240]{2,1,0:T(8,128)(2,1)S(1)}, bf16[2,80,240]{2,1,0:T(8,128)(2,1)S(1)}, u32[]{:S(2)}, u32[]{:S(2)}) collective-permute-start(bf16[2,80,240]{2,1,0:T(8,128)(2,1)S(1)} %pad_maximum_fusion.39), channel_id=1, source_target_pairs={{0,2},{2,0},{1,3},{3,1},{4,6},{6,4},{5,7},{7,5},{8,10},{10,8},{9,1... | collective-permute-start | bytes 230408 | tf_op jit(solution)/shard_map/ppermute | solution.py:52
  41.1 28.7 %collective-permute-start.50 = (bf16[2,4,30,640]{3,0,2,1:T(2,128)(2,1)S(1)}, bf16[2,4,30,640]{3,0,2,1:T(2,128)(2,1)S(1)}, u32[]{:S(2)}, u32[]{:S(2)}) collective-permute-start(bf16[2,4,30,640]{3,0,2,1:T(2,128)(2,1)S(1)} %copy_dynamic-update-slice_fusion.15), channel_id=1, source_target_pairs={{0,16},{16,0},{1,17},{17,1},{2,18},{18,2},{3,19},{19,3},{4,20},{20... | collective-permute-start | bytes 921608 | tf_op jit(solution)/shard_map/ppermute | solution.py:52
  42.1 34.3 %collective-permute-start.38 = (bf16[2,2,80,480]{3,2,0,1:T(8,128)(2,1)S(1)}, bf16[2,2,80,480]{3,2,0,1:T(8,128)(2,1)S(1)}, u32[]{:S(2)}, u32[]{:S(2)}) collective-permute-start(bf16[2,2,80,480]{3,2,0,1:T(8,128)(2,1)S(1)} %get-tuple-element.122), channel_id=1, source_target_pairs={{0,96},{32,0},{64,32},{96,64},{1,97},{33,1},{65,33},{97,65},{2,98}... | collective-permute-start | bytes 921608 | tf_op jit(solution)/shard_map/ppermute | solution.py:52
  52.3 24.8 %collective-permute-start.39 = (bf16[2,2,80,480]{3,2,0,1:T(8,128)(2,1)S(1)}, bf16[2,2,80,480]{3,2,0,1:T(8,128)(2,1)S(1)}, u32[]{:S(2)}, u32[]{:S(2)}) collective-permute-start(bf16[2,2,80,480]{3,2,0,1:T(8,128)(2,1)S(1)} %get-tuple-element.122), channel_id=1, source_target_pairs={{0,64},{32,96},{64,0},{96,32},{1,65},{33,97},{65,1},{97,33},{2,66}... | collective-permute-start | bytes 921608 | tf_op jit(solution)/shard_map/ppermute | solution.py:52
  66.4 24.7 %collective-permute-start.31 = (bf16[2,240,480]{2,0,1:T(2,128)(2,1)S(1)}, bf16[2,240,480]{2,0,1:T(2,128)(2,1)}, u32[]{:S(2)}, u32[]{:S(2)}) collective-permute-start(bf16[2,240,480]{2,0,1:T(2,128)(2,1)S(1)} %bitcast.653), channel_id=1, source_target_pairs={{0,96},{32,0},{64,32},{96,64},{1,97},{33,1},{65,33},{97,65},{2,98}... | collective-permute-start | bytes 1382408 | tf_op jit(solution)/shard_map/ppermute | solution.py:52
  77.1 47.8 %collective-permute-start.51 = (bf16[2,240,640]{2,0,1:T(2,128)(2,1)}, bf16[2,240,640]{2,0,1:T(2,128)(2,1)S(1)}, u32[]{:S(2)}, u32[]{:S(2)}) collective-permute-start(bf16[2,240,640]{2,0,1:T(2,128)(2,1)} %bitcast.89), channel_id=1, source_target_pairs={{0,96},{32,0},{64,32},{96,64},{1,97},{33,1},{65,33},{97,65},{2,98}... | collective-permute-start | bytes 1843208 | tf_op jit(solution)/shard_map/ppermute | solution.py:52
  80.4 42.6 %collective-permute-start.53 = (bf16[2,240,640]{2,0,1:T(2,128)(2,1)}, bf16[2,240,640]{2,0,1:T(2,128)(2,1)}, u32[]{:S(2)}, u32[]{:S(2)}) collective-permute-start(bf16[2,240,640]{2,0,1:T(2,128)(2,1)} %bitcast.89), channel_id=1, source_target_pairs={{0,32},{32,64},{64,96},{96,0},{1,33},{33,65},{65,97},{97,1},{2,34}... | collective-permute-start | bytes 1843208 | tf_op jit(solution)/shard_map/ppermute | solution.py:52
  86.7 65.2 %collective-permute-start.41 = (bf16[2,4,2,80,480]{4,3,2,1,0:T(8,128)(2,1)}, bf16[2,4,2,80,480]{4,3,2,1,0:T(8,128)(2,1)S(1)}, u32[]{:S(2)}, u32[]{:S(2)}) collective-permute-start(bf16[2,4,2,80,480]{4,3,2,1,0:T(8,128)(2,1)} %copy_dynamic-update-slice_fusion.7), channel_id=1, source_target_pairs={{0,12},{4,0},{8,4},{12,8},{1,13},{5,1},{9,5},{13,9},{2,14},{6,2},{... | collective-permute-start | bytes 3686408 | tf_op jit(solution)/shard_map/ppermute | solution.py:52
  130.0 30.3 %collective-permute-start.43 = (bf16[2,4,2,80,480]{4,3,2,1,0:T(8,128)(2,1)}, bf16[2,4,2,80,480]{4,3,2,1,0:T(8,128)(2,1)S(1)}, u32[]{:S(2)}, u32[]{:S(2)}) collective-permute-start(bf16[2,4,2,80,480]{4,3,2,1,0:T(8,128)(2,1)} %copy_dynamic-update-slice_fusion.7), channel_id=1, source_target_pairs={{0,4},{4,8},{8,12},{12,0},{1,5},{5,9},{9,13},{13,1},{2,6},{6,10},{... | collective-permute-start | bytes 3686408 | tf_op jit(solution)/shard_map/ppermute | solution.py:52
  131.9 73.6 %collective-permute-start.35 = (bf16[2,960,480]{2,1,0:T(8,128)(2,1)}, bf16[2,960,480]{2,1,0:T(8,128)(2,1)}, u32[]{:S(2)}, u32[]{:S(2)}) collective-permute-start(bf16[2,960,480]{2,1,0:T(8,128)(2,1)} %bitcast.44), channel_id=1, source_target_pairs={{0,1},{1,0},{2,3},{3,2},{4,5},{5,4},{6,7},{7,6},{8,9},{9,8},{10,11... | collective-permute-start | bytes 5529608 | tf_op jit(solution)/shard_map/ppermute | solution.py:52
  149.3 20.1 %collective-permute-start.19 = (bf16[128,640]{1,0:T(8,128)(2,1)S(1)}, bf16[128,640]{1,0:T(8,128)(2,1)S(1)}, u32[]{:S(2)}, u32[]{:S(2)}) collective-permute-start(bf16[128,640]{1,0:T(8,128)(2,1)S(1)} %pad_maximum_fusion.26), channel_id=1, source_target_pairs={{0,96},{32,0},{64,32},{96,64},{1,97},{33,1},{65,33},{97,65},{2,98}... | collective-permute-start | bytes 491528 | tf_op jit(solution)/shard_map/ppermute | solution.py:52
  170.0 78.7 %collective-permute-start.55 = (bf16[2,960,640]{2,1,0:T(8,128)(2,1)}, bf16[2,960,640]{2,1,0:T(8,128)(2,1)}, u32[]{:S(2)}, u32[]{:S(2)}) collective-permute-start(bf16[2,960,640]{2,1,0:T(8,128)(2,1)} %bitcast.95), channel_id=1, source_target_pairs={{0,1},{1,0},{2,3},{3,2},{4,5},{5,4},{6,7},{7,6},{8,9},{9,8},{10,11... | collective-permute-start | bytes 7372808 | tf_op jit(solution)/shard_map/ppermute | solution.py:52
  177.0 20.2 %collective-permute-start.22 = (bf16[512,640]{1,0:T(8,128)(2,1)}, bf16[512,640]{1,0:T(8,128)(2,1)}, u32[]{:S(2)}, u32[]{:S(2)}) collective-permute-start(bf16[512,640]{1,0:T(8,128)(2,1)} %get-tuple-element.178), channel_id=1, source_target_pairs={{0,12},{4,0},{8,4},{12,8},{1,13},{5,1},{9,5},{13,9},{2,14},{6,2},{... | collective-permute-start | bytes 1966088 | tf_op jit(solution)/shard_map/ppermute | solution.py:52
  179.4 23.3 %collective-permute-start.24 = (bf16[512,640]{1,0:T(8,128)(2,1)}, bf16[512,640]{1,0:T(8,128)(2,1)S(1)}, u32[]{:S(2)}, u32[]{:S(2)}) collective-permute-start(bf16[512,640]{1,0:T(8,128)(2,1)} %get-tuple-element.178), channel_id=1, source_target_pairs={{0,4},{4,8},{8,12},{12,0},{1,5},{5,9},{9,13},{13,1},{2,6},{6,10},{... | collective-permute-start | bytes 1966088 | tf_op jit(solution)/shard_map/ppermute | solution.py:52
  191.8 60.7 %collective-permute-start.45 = (bf16[2,2560,480]{1,2,0:T(8,128)(2,1)}, bf16[2,2560,480]{1,2,0:T(8,128)(2,1)}, u32[]{:S(2)}, u32[]{:S(2)}) collective-permute-start(bf16[2,2560,480]{1,2,0:T(8,128)(2,1)} %copy.345), channel_id=1, source_target_pairs={{0,1},{1,0},{2,3},{3,2},{4,5},{5,4},{6,7},{7,6},{8,9},{9,8},{10,11... | collective-permute-start | bytes 14745608 | tf_op jit(solution)/shard_map/ppermute | solution.py:52
  312.1 31.8 %collective-permute-start.56 = (bf16[256,640]{1,0:T(8,128)(2,1)S(1)}, bf16[256,640]{1,0:T(8,128)(2,1)S(1)}, u32[]{:S(2)}, u32[]{:S(2)}) collective-permute-start(bf16[256,640]{1,0:T(8,128)(2,1)S(1)} %get-tuple-element.42), channel_id=1, source_target_pairs={{0,32},{32,64},{64,96},{96,0},{1,33},{33,65},{65,97},{97,1},{2,34}... | collective-permute-start | bytes 983048 | tf_op jit(solution)/shard_map/ppermute | solution.py:52
  312.2 35.0 %collective-permute-start.66 = (bf16[256,640]{1,0:T(8,128)(2,1)S(1)}, bf16[256,640]{1,0:T(8,128)(2,1)S(1)}, u32[]{:S(2)}, u32[]{:S(2)}) collective-permute-start(bf16[256,640]{1,0:T(8,128)(2,1)S(1)} %get-tuple-element.43), channel_id=1, source_target_pairs={{0,12},{4,0},{8,4},{12,8},{1,13},{5,1},{9,5},{13,9},{2,14},{6,2},{... | collective-permute-start | bytes 983048 | tf_op jit(solution)/shard_map/ppermute | solution.py:52
  313.6 34.5 %collective-permute-start.64 = (bf16[256,640]{1,0:T(8,128)(2,1)S(1)}, bf16[256,640]{1,0:T(8,128)(2,1)S(1)}, u32[]{:S(2)}, u32[]{:S(2)}) collective-permute-start(bf16[256,640]{1,0:T(8,128)(2,1)S(1)} %get-tuple-element.46), channel_id=1, source_target_pairs={{0,4},{4,8},{8,12},{12,0},{1,5},{5,9},{9,13},{13,1},{2,6},{6,10},{... | collective-permute-start | bytes 983048 | tf_op jit(solution)/shard_map/ppermute | solution.py:52
  314.3 33.7 %collective-permute-start.58 = (bf16[256,640]{1,0:T(8,128)(2,1)S(1)}, bf16[256,640]{1,0:T(8,128)(2,1)S(1)}, u32[]{:S(2)}, u32[]{:S(2)}) collective-permute-start(bf16[256,640]{1,0:T(8,128)(2,1)S(1)} %get-tuple-element.47), channel_id=1, source_target_pairs={{0,96},{32,0},{64,32},{96,64},{1,97},{33,1},{65,33},{97,65},{2,98}... | collective-permute-start | bytes 983048 | tf_op jit(solution)/shard_map/ppermute | solution.py:52
  348.5 26.9 %collective-permute-start.59 = (bf16[512,640]{1,0:T(8,128)(2,1)S(1)}, bf16[512,640]{1,0:T(8,128)(2,1)S(1)}, u32[]{:S(2)}, u32[]{:S(2)}) collective-permute-start(bf16[512,640]{1,0:T(8,128)(2,1)S(1)} %pad_maximum_fusion.9), channel_id=1, source_target_pairs={{0,96},{32,0},{64,32},{96,64},{1,97},{33,1},{65,33},{97,65},{2,98}... | collective-permute-start | bytes 1966088 | tf_op jit(solution)/shard_map/ppermute | solution.py:52
  350.6 25.3 %collective-permute-start.57 = (bf16[512,640]{1,0:T(8,128)(2,1)S(1)}, bf16[512,640]{1,0:T(8,128)(2,1)S(1)}, u32[]{:S(2)}, u32[]{:S(2)}) collective-permute-start(bf16[512,640]{1,0:T(8,128)(2,1)S(1)} %pad_maximum_fusion.8), channel_id=1, source_target_pairs={{0,32},{32,64},{64,96},{96,0},{1,33},{33,65},{65,97},{97,1},{2,34}... | collective-permute-start | bytes 1966088 | tf_op jit(solution)/shard_map/ppermute | solution.py:52
  350.9 25.0 %collective-permute-start.67 = (bf16[512,640]{1,0:T(8,128)(2,1)S(1)}, bf16[512,640]{1,0:T(8,128)(2,1)S(1)}, u32[]{:S(2)}, u32[]{:S(2)}) collective-permute-start(bf16[512,640]{1,0:T(8,128)(2,1)S(1)} %pad_maximum_fusion.11), channel_id=1, source_target_pairs={{0,12},{4,0},{8,4},{12,8},{1,13},{5,1},{9,5},{13,9},{2,14},{6,2},{... | collective-permute-start | bytes 1966088 | tf_op jit(solution)/shard_map/ppermute | solution.py:52
  351.6 24.2 %collective-permute-start.65 = (bf16[512,640]{1,0:T(8,128)(2,1)S(1)}, bf16[512,640]{1,0:T(8,128)(2,1)S(1)}, u32[]{:S(2)}, u32[]{:S(2)}) collective-permute-start(bf16[512,640]{1,0:T(8,128)(2,1)S(1)} %pad_maximum_fusion.10), channel_id=1, source_target_pairs={{0,4},{4,8},{8,12},{12,0},{1,5},{5,9},{9,13},{13,1},{2,6},{6,10},{... | collective-permute-start | bytes 1966088 | tf_op jit(solution)/shard_map/ppermute | solution.py:52
  374.7 64.6 %collective-permute-start.81 = (bf16[2,960,480]{2,1,0:T(8,128)(2,1)}, bf16[2,960,480]{2,1,0:T(8,128)(2,1)}, u32[]{:S(2)}, u32[]{:S(2)}) collective-permute-start(bf16[2,960,480]{2,1,0:T(8,128)(2,1)} %pad_maximum_fusion.2), channel_id=1, source_target_pairs={{0,1},{1,0},{2,3},{3,2},{4,5},{5,4},{6,7},{7,6},{8,9},{9,8},{10,11... | collective-permute-start | bytes 5529608 | tf_op jit(solution)/shard_map/ppermute | solution.py:52
  375.3 119.4 %collective-permute-start.110 = (bf16[2,2560,480]{1,2,0:T(8,128)(2,1)}, bf16[2,2560,480]{1,2,0:T(8,128)(2,1)}, u32[]{:S(2)}, u32[]{:S(2)}) collective-permute-start(bf16[2,2560,480]{1,2,0:T(8,128)(2,1)} %pad_maximum_fusion), channel_id=1, source_target_pairs={{0,1},{1,0},{2,3},{3,2},{4,5},{5,4},{6,7},{7,6},{8,9},{9,8},{10,11... | collective-permute-start | bytes 14745608 | tf_op jit(solution)/shard_map/ppermute | solution.py:52
  428.9 46.7 %collective-permute-start.120 = (bf16[2,960,640]{2,1,0:T(8,128)(2,1)S(1)}, bf16[2,960,640]{2,1,0:T(8,128)(2,1)S(1)}, u32[]{:S(2)}, u32[]{:S(2)}) collective-permute-start(bf16[2,960,640]{2,1,0:T(8,128)(2,1)S(1)} %copy-done.33), channel_id=1, source_target_pairs={{0,1},{1,0},{2,3},{3,2},{4,5},{5,4},{6,7},{7,6},{8,9},{9,8},{10,11... | collective-permute-start | bytes 7372808 | tf_op jit(solution)/shard_map/ppermute | solution.py:52
  490.1 43.7 %collective-permute-start.124 = (bf16[2,240,640]{2,1,0:T(8,128)(2,1)}, bf16[2,240,640]{2,1,0:T(8,128)(2,1)S(1)}, u32[]{:S(2)}, u32[]{:S(2)}) collective-permute-start(bf16[2,240,640]{2,1,0:T(8,128)(2,1)} %pad_maximum_fusion.15), channel_id=1, source_target_pairs={{0,96},{32,0},{64,32},{96,64},{1,97},{33,1},{65,33},{97,65},{2,98}... | collective-permute-start | bytes 1843208 | tf_op jit(solution)/shard_map/ppermute | solution.py:52
  494.7 39.1 %collective-permute-start.122 = (bf16[2,240,640]{2,1,0:T(8,128)(2,1)}, bf16[2,240,640]{2,1,0:T(8,128)(2,1)}, u32[]{:S(2)}, u32[]{:S(2)}) collective-permute-start(bf16[2,240,640]{2,1,0:T(8,128)(2,1)} %pad_maximum_fusion.14), channel_id=1, source_target_pairs={{0,32},{32,64},{64,96},{96,0},{1,33},{33,65},{65,97},{97,1},{2,34}... | collective-permute-start | bytes 1843208 | tf_op jit(solution)/shard_map/ppermute | solution.py:52
  510.4 18.9 %collective-permute-start.111 = (bf16[1,4,2,80,480]{4,3,2,1,0:T(8,128)(2,1)S(1)}, bf16[1,4,2,80,480]{4,3,2,1,0:T(8,128)(2,1)S(1)}, u32[]{:S(2)}, u32[]{:S(2)}) collective-permute-start(bf16[1,4,2,80,480]{4,3,2,1,0:T(8,128)(2,1)S(1)} %get-tuple-element.33), channel_id=1, source_target_pairs={{0,4},{4,8},{8,12},{12,0},{1,5},{5,9},{9,13},{13,1},{2,6},{6,10},{... | collective-permute-start | bytes 1843208 | tf_op jit(solution)/shard_map/ppermute | solution.py:52
  513.8 24.4 %collective-permute-start.90 = (bf16[2,30,240]{2,1,0:T(8,128)(2,1)S(1)}, bf16[2,30,240]{2,1,0:T(8,128)(2,1)S(1)}, u32[]{:S(2)}, u32[]{:S(2)}) collective-permute-start(bf16[2,30,240]{2,1,0:T(8,128)(2,1)S(1)} %broadcast_select_fusion.31), channel_id=1, source_target_pairs={{0,2},{2,0},{1,3},{3,1},{4,6},{6,4},{5,7},{7,5},{8,10},{10,8},{9,1... | collective-permute-start | bytes 86408 | tf_op jit(solution)/shard_map/ppermute | solution.py:52
  533.5 20.0 %collective-permute-start.112 = (bf16[2,4,2,80,480]{4,3,2,1,0:T(8,128)(2,1)S(1)}, bf16[2,4,2,80,480]{4,3,2,1,0:T(8,128)(2,1)S(1)}, u32[]{:S(2)}, u32[]{:S(2)}) collective-permute-start(bf16[2,4,2,80,480]{4,3,2,1,0:T(8,128)(2,1)S(1)} %pad_maximum_fusion.4), channel_id=1, source_target_pairs={{0,4},{4,8},{8,12},{12,0},{1,5},{5,9},{9,13},{13,1},{2,6},{6,10},{... | collective-permute-start | bytes 3686408 | tf_op jit(solution)/shard_map/ppermute | solution.py:52
  (178 other events, 1714.9 us)
